TPU v7x, 32 devices: a whole 2x2x4 slice. The times are simulated.
32 devices in a mesh: dp: 4 (over z), mp: 8 (over y, x, core).
Axes of the slice: x: 2, y: 2, z: 4, core: 2. Of those that a mesh axis runs over, the one named last changes fastest.
Arguments:
- inputs: bfloat16 [2, 37632, 1024], P(None, ('dp', 'mp')), may hold values from -6 to 6
- norm0_gain: float32 [1024], replicated, may hold values from 0.5 to 1.5
- norm0_bias: float32 [1024], replicated, may hold values from -1.75 to 1.75
- merge_weight: bfloat16 [1024, 512], replicated, may hold values from -0.1875 to 0.1875
- norm1_gain: float32 [512], replicated, may hold values from 0.5 to 1.5
- norm1_bias: float32 [512], replicated, may hold values from -1.75 to 1.75
- qkv_weight: bfloat16 [512, 16, 96], P(None, 'mp'), may hold values from -0.25 to 0.25
- qkv_bias: bfloat16 [16, 96], P('mp'), may hold values from -1.75 to 1.75
- rel_table: bfloat16 [16, 169], P('mp'), may hold values from -4 to 4
- rel_index: int32 [49, 49], replicated, may hold values from 0 to 168
- regions: int32 [2, 37632], P(None, 'dp'), may hold values from 0 to 3, as said below
- live_windows: int32 [2, 4], P(None, 'dp'), may hold values from 96 to 192, as said below
- proj_weight: bfloat16 [16, 32, 512], P('mp'), may hold values from -0.75 to 0.75
- proj_bias: float32 [512], replicated, may hold values from -1.75 to 1.75
- norm2_gain: float32 [512], replicated, may hold values from 0.5 to 1.5
- norm2_bias: float32 [512], replicated, may hold values from -1.75 to 1.75
- up_weight: bfloat16 [512, 2048], P(None, 'mp'), may hold values from -0.25 to 0.25
- up_bias: bfloat16 [2048], P('mp'), may hold values from -1.75 to 1.75
- down_weight: bfloat16 [2048, 512], P('mp'), may hold values from -0.125 to 0.125
- down_bias: float32 [512], replicated, may hold values from -1.75 to 1.75
- cotangent: bfloat16 [2, 37632, 512], P(None, ('dp', 'mp')), may hold values from -6 to 6
Outputs:
- output: float32 [2, 37632, 512], P(None, ('dp', 'mp'))
- grad_input: float32 [2, 37632, 1024], P(None, ('dp', 'mp'))
- grad_norm0_gain: float32 [1024], replicated
- grad_norm0_bias: float32 [1024], replicated
- grad_merge: float32 [1024, 512], replicated
- grad_norm1_gain: float32 [512], replicated
- grad_norm1_bias: float32 [512], replicated
- grad_qkv: float32 [512, 16, 96], P(None, 'mp')
- grad_qkv_bias: float32 [16, 96], P('mp')
- grad_rel_table: float32 [16, 169], P('mp')
- grad_proj: float32 [16, 32, 512], P('mp')
- grad_proj_bias: float32 [512], replicated
- grad_norm2_gain: float32 [512], replicated
- grad_norm2_bias: float32 [512], replicated
- grad_up: float32 [512, 2048], P(None, 'mp')
- grad_up_bias: float32 [2048], P('mp')
- grad_down: float32 [2048, 512], P('mp')
- grad_down_bias: float32 [512], replicated
Inputs may be any that keep to these rules, and one draw needn't show every extreme that they name: `regions`: in every window the region ids of its positions are 2 * (row >= r) + (column >= c) for that window's cuts r, c from 0 to 6; the first window of each micro-batch is cut both ways. `live_windows`: for every page group some micro-batch has all 192 windows live; live windows are the first ones of their group.
All inputs are finite; a program needn't handle non-finite values.
Results may differ from a plain program's by a relative error of at most 0.018.
Values may be sent and summed in bfloat16 or wider, within the bound.
A program may use at most 256 MiB of HBM per device.

v0:
```python
import functools
import math

import jax
import jax.numpy as jnp
from jax import lax
from jax.experimental import pallas as pl
from jax.experimental.pallas import tpu as pltpu
from jax.sharding import PartitionSpec as P

F32 = jnp.float32
BF16 = jnp.bfloat16
EPSILON = 1e-05
MASKED = -1e30
COVER = 64
TILE = 16
GROUP = 4
VMEM_LIMIT = 60 << 20


def dot(left, right):
    return jnp.dot(left, right, preferred_element_type=F32)


def dot_rt(left, right):
    return lax.dot_general(left, right, (((1,), (1,)), ((), ())), preferred_element_type=F32)


def dot_lt(left, right):
    return lax.dot_general(left, right, (((0,), (0,)), ((), ())), preferred_element_type=F32)


def whole(shape):
    return pl.BlockSpec(shape, lambda i: (0,) * len(shape), pipeline_mode=pl.Buffered(1))


def anywhere():
    return pl.BlockSpec(memory_space=pl.ANY)


def call(kernel, grid, ins, in_specs, outs, out_specs, scratch, flops, nbytes, group=None):
    extra = {} if group is None else {"collective_id": group, "has_side_effects": True}
    return pl.pallas_call(
        kernel,
        grid=(grid,),
        in_specs=in_specs,
        out_specs=out_specs,
        out_shape=outs,
        scratch_shapes=scratch,
        compiler_params=pltpu.CompilerParams(
            dimension_semantics=("arbitrary",), vmem_limit_bytes=VMEM_LIMIT, **extra
        ),
        cost_estimate=pl.CostEstimate(flops=flops, bytes_accessed=nbytes, transcendentals=0),
    )(*ins)


def partner(axis, flips):
    at = lax.axis_index(axis)
    bit = 1
    while bit <= flips:
        if flips & bit:
            at = at + bit * (1 - 2 * lax.rem(lax.div(at, jnp.int32(bit)), jnp.int32(2)))
        bit *= 2
    return at


def send(axis, flips, src, dst, send_sem, recv_sem):
    return pltpu.make_async_remote_copy(
        src_ref=src,
        dst_ref=dst,
        send_sem=send_sem,
        recv_sem=recv_sem,
        device_id={axis: partner(axis, flips)},
        device_id_type=pl.DeviceIdType.MESH,
    )


def greet(peers):
    barrier = pltpu.get_barrier_semaphore()
    for axis, flips in peers:
        pl.semaphore_signal(
            barrier,
            inc=1,
            device_id={axis: partner(axis, flips)},
            device_id_type=pl.DeviceIdType.MESH,
        )
    pl.semaphore_wait(barrier, len(peers))


class Gather:
    def __init__(self, axis, size, own, held, send_sems, recv_sems, own_sem):
        self.axis, self.size, self.own, self.held = axis, size, own, held
        self.send_sems, self.recv_sems, self.own_sem = send_sems, recv_sems, own_sem

    def straight(self, r):
        return send(
            self.axis, r, self.own, self.held.at[r], self.send_sems.at[r], self.recv_sems.at[r]
        )

    def onward(self, r):
        return send(
            self.axis,
            1,
            self.held.at[r],
            self.held.at[r + 1],
            self.send_sems.at[r + 1],
            self.recv_sems.at[r + 1],
        )

    def keep(self):
        return pltpu.make_async_copy(self.own, self.held.at[0], self.own_sem)

    def start(self, flips=None):
        evens = list(range(2, self.size, 2))
        for r in evens + [1] if flips is None else flips:
            self.straight(r).start()
        if flips is None or 1 in flips:
            self.keep().start()

    def forward(self, r):
        self.straight(r).wait_recv()
        self.onward(r).start()

    def finish(self):
        self.keep().wait()
        self.straight(1).wait()
        for r in range(2, self.size, 2):
            self.straight(r).wait_send()
            self.onward(r).wait()


def spans(total, step):
    return [(start, min(step, total - start)) for start in range(0, total, step)]


def norm_parts(values):
    mean = jnp.mean(values, axis=-1, keepdims=True)
    center = values - mean
    spread = jnp.mean(center * center, axis=-1, keepdims=True) + EPSILON
    inverse = lax.rsqrt(spread)
    return center * inverse, mean, inverse, spread


def norm_back(grad, normed, inverse):
    mean_grad = jnp.mean(grad, axis=-1, keepdims=True)
    mean_cross = jnp.mean(grad * normed, axis=-1, keepdims=True)
    return inverse * (grad - mean_grad - normed * mean_cross)


def head_mask(head_dim):
    rows = lax.broadcasted_iota(jnp.int32, (GROUP * COVER, GROUP * head_dim), 0) // COVER
    cols = lax.broadcasted_iota(jnp.int32, (GROUP * COVER, GROUP * head_dim), 1) // head_dim
    return (rows == cols).astype(F32).astype(BF16)


def tiled(block, mask):
    return jnp.concatenate([block] * GROUP, axis=0) * mask


def pair_row(idx_ref, pair):
    win = idx_ref.shape[0]
    gap = jnp.full((1, COVER - win), -1, jnp.int32)
    parts = []
    for i in (2 * pair, 2 * pair + 1):
        parts.append(idx_ref[i : i + 1, :] if i < win else jnp.full((1, win), -1, jnp.int32))
        parts.append(gap)
    return jnp.concatenate(parts, axis=1)


def index_onehot(row, table_width):
    entry = lax.broadcasted_iota(jnp.int32, (table_width, row.shape[1]), 0)
    return (entry == row).astype(F32).astype(BF16)


def fill(x, width):
    return jnp.concatenate([x, jnp.zeros((x.shape[0], width - x.shape[1]), x.dtype)], axis=1)


def front_kernel(
    head_dim,
    local,
    size,
    merge_steps,
    x_ref,
    g0_ref,
    b0_ref,
    wm_ref,
    g1_ref,
    b1_ref,
    qkvw_ref,
    qkvb_ref,
    tab_ref,
    ub_ref,
    up_ref,
    down_ref,
    proj_ref,
    idx_ref,
    rid_ref,
    stats_ref,
    n1_ref,
    q_ref,
    k_ref,
    v_ref,
    att_ref,
    rinv_ref,
    p_ref,
    tiles_ref,
    wt_ref,
    second_ref,
    first_s,
    tiles_s,
    own_s,
    tile_s,
    second_s,
    mid_s,
    q_s,
    k_s,
    v_s,
    att_s,
    rinv_s,
    base_s,
    bias_s,
    mask_s,
    tile_send,
    tile_recv,
    first_send,
    first_recv,
    second_send,
    second_recv,
    own_sems,
    out_sems,
):
    step = pl.program_id(0)
    rows, width = mid_s.shape
    heads = width // head_dim
    lanes = GROUP * head_dim
    groups = heads // GROUP
    per_group = size // groups
    scale = 1.0 / math.sqrt(head_dim)
    span = local * head_dim
    evens = list(range(2, size, 2))
    main = Gather("mp", size, own_s, first_s, first_send, first_recv, own_sems.at[0])
    rest = Gather("mp", size, second_s, second_ref, second_send, second_recv, own_sems.at[1])

    def tile_copy(r):
        return send("mp", r, tile_s, tiles_s.at[r], tile_send.at[r], tile_recv.at[r])

    @pl.when(step == 0)
    def _():
        own_s[...] = qkvw_ref[...].T
        bias = qkvb_ref[...].astype(F32)
        lines = []
        for t in range(3):
            parts = [
                bias[l : l + 1, t * head_dim : (t + 1) * head_dim] for l in range(local)
            ]
            lines.append(fill(jnp.concatenate(parts, axis=1), width))
        lines.append(fill(tab_ref[...].astype(F32), width))
        lines.append(fill(ub_ref[...].astype(F32), width))
        lines.append(jnp.zeros((TILE - 4 - local, width), F32))
        tile_s[...] = jnp.concatenate(lines, axis=0).astype(BF16)
        greet([("mp", r) for r in range(1, size)])
        for r in range(1, size):
            tile_copy(r).start()
        tiles_s[0] = tile_s[...]
        main.start([r for r in evens if r < 2 * per_group] + [1])
        hidden = up_ref.shape[1]
        second_s[:hidden, :] = up_ref[...].T
        second_s[hidden : 2 * hidden, :] = down_ref[...]
        second_s[2 * hidden :, :] = proj_ref[...]

    @pl.when(step == 2)
    def _():
        main.start([r for r in evens if r >= 2 * per_group])

    @pl.when(step == merge_steps - 3)
    def _():
        rest.start()

    @pl.when(step < merge_steps)
    def _():
        count = x_ref.shape[0]
        here = pl.ds(pl.multiple_of(step * count, TILE), count)
        normed, mean, inverse, _ = norm_parts(x_ref[...].astype(F32))
        normed_in = (normed * g0_ref[...] + b0_ref[...]).astype(BF16)
        normed1, mean1, inverse1, spread1 = norm_parts(dot(normed_in, wm_ref[...]))
        n1_ref[...] = normed1.astype(BF16)
        stats = [mean, inverse, mean1, inverse1, spread1 * inverse1]
        stats_ref[...] = jnp.concatenate(stats + [mean] * (8 - len(stats)), axis=1)
        mid_s[here, :] = (normed1 * g1_ref[...] + b1_ref[...]).astype(BF16)

    table_step = merge_steps - 3

    @pl.when(step == merge_steps - 1)
    def _():
        for r in evens:
            if r < 2 * per_group:
                main.forward(r)

    @pl.when(step == table_step)
    def _():
        mask_s[...] = head_mask(head_dim)
        att_s[...] = jnp.zeros_like(att_s)
        rinv_s[...] = jnp.zeros_like(rinv_s)
        base_s[...] = jnp.full(base_s.shape, MASKED, F32)
        for r in range(1, size):
            tile_copy(r).wait_recv()

    all_pairs = list(range((idx_ref.shape[0] + 1) // 2))
    for i in range(2):

        @pl.when(step == table_step + i)
        def _():
            table = jnp.concatenate(
                [tiles_s[r].astype(F32)[3 : 3 + local, : 2 * 128] for r in range(size)], axis=0
            ).astype(BF16)
            here = all_pairs[i::2]
            rows_of = [pair_row(idx_ref, pair) for pair in here]
            found = [dot(table, index_onehot(row, table.shape[1])) for row in rows_of]
            found = [jnp.where(row < 0, MASKED, x) for row, x in zip(rows_of, found)]
            for pair, vals in zip(here, found):
                base_s[:, 2 * pair, :] = vals[:, :COVER]
                base_s[:, 2 * pair + 1, :] = vals[:, COVER:]

    @pl.when(step == table_step + 2)
    def _():
        tiles_ref[...] = tiles_s[...]

        def shift(g, _):
            full = jnp.concatenate([base_s[g * GROUP + h] for h in range(GROUP)], axis=1)
            for o in range(TILE):
                bias_s[g, o] = pltpu.roll(pltpu.roll(full, o, 0), o, 1) if o else full
            return 0

        lax.fori_loop(0, groups, shift, 0)
        for r in range(1, size):
            tile_copy(r).wait_send()

    def outward(ref, out, which, g):
        cols = pl.ds(pl.multiple_of(g * lanes, lanes), lanes)
        return pltpu.make_async_copy(ref.at[:, cols], out.at[:, cols], out_sems.at[which, g])

    def early_out(g):
        return [
            outward(ref, out, i, g)
            for i, (ref, out) in enumerate(((q_s, q_ref), (k_s, k_ref), (v_s, v_ref)))
        ]

    def late_out(g):
        return [outward(att_s, att_ref, 3, g), outward(rinv_s, rinv_ref, 4, g)]

    low_half = lax.broadcasted_iota(jnp.int32, (COVER, 2 * COVER), 1) < COVER
    region_of = lax.broadcasted_iota(jnp.int32, (8, GROUP * COVER), 0)
    sets = rid_ref.shape[1]
    block = rows // sets

    def attend(it, g):
        mask = mask_s[...]
        cols = pl.ds(pl.multiple_of(g * lanes, lanes), lanes)
        units = [(2 * it + i, u) for i in range(2) for u in range(sets)]
        starts = [pl.multiple_of(o * (block // TILE - 1) + u * block, TILE) for o, u in units]
        scores = []
        for start in starts:
            here = pl.ds(start, COVER)
            scores.append(dot_rt(q_s[here, cols], tiled(k_s[here, cols], mask)))
        weights = []
        for (o, u), s in zip(units, scores):
            member = (region_of == rid_ref[o, u]).astype(F32).astype(BF16)
            same = dot_lt(member[:, :COVER], member)
            s = s + bias_s[g, o] + jnp.where(same > 0.5, 0.0, MASKED)
            parts = []
            for c in range(GROUP // 2):
                x = s[:, c * 2 * COVER : (c + 1) * 2 * COVER]
                top0 = jnp.max(jnp.where(low_half, x, MASKED), axis=1, keepdims=True)
                top1 = jnp.max(jnp.where(low_half, MASKED, x), axis=1, keepdims=True)
                top = jnp.maximum(jnp.where(low_half, top0, top1), MASKED * 0.1)
                parts.append(jnp.exp(x - top).astype(BF16))
            w = jnp.concatenate(parts, axis=1)
            p_ref[0, o, u] = w
            weights.append(w)
        mixed = []
        for start, w in zip(starts, weights):
            vals = tiled(v_s[pl.ds(start, COVER), cols], mask)
            mixed.append(dot(w, jnp.concatenate([vals, mask], axis=1)))
        for start, a in zip(starts, mixed):
            here = pl.ds(start, COVER)
            total = a[:, lanes:]
            inv = jnp.where(total > 0.0, 1.0 / jnp.maximum(total, 0.5), 0.0)
            att_s[here, cols] += (a[:, :lanes] * inv).astype(BF16)
            rinv_s[here, cols] += inv.astype(BF16)

    @pl.when(step >= merge_steps)
    def _():
        g = step - merge_steps
        twice = 2 * per_group

        @pl.when(g == 0)
        def _():
            main.keep().wait()
            main.straight(1).wait_recv()
            for r in evens:
                if r < twice:
                    main.onward(r).wait_recv()

        for known in range(2, groups, 2):

            @pl.when(g == known)
            def _():
                for r in evens:
                    if known * per_group <= r < known * per_group + twice:
                        main.onward(r).wait_recv()

        @pl.when(g % 2 == 0)
        def _():
            shards = [g * per_group + j for j in range(twice)]
            cols = pl.ds(pl.multiple_of(g * lanes, 2 * lanes), 2 * lanes)
            outs = (q_s, k_s, v_s)
            part = rows // 3
            weights, biases = [], []
            for t in range(3):
                weight = []
                for s in shards:
                    for l in range(local):
                        at = (3 * l + t) * head_dim
                        weight.append(first_s[s, at : at + head_dim, :])
                    biases.append(tiles_s[s].astype(F32)[t : t + 1, :span])
                weight = jnp.concatenate(weight, axis=0)
                spot = pl.ds(pl.multiple_of(t * width + g * lanes, 2 * lanes), 2 * lanes)
                wt_ref[spot, :] = weight
                weights.append(weight.T)
            weight = jnp.concatenate(weights, axis=1)
            bias = jnp.concatenate(biases, axis=1)

            def project(i, _):
                here = pl.ds(pl.multiple_of(i * part, TILE), part)
                y = dot(mid_s[here, :], weight) + bias
                for t in range(3):
                    z = y[:, 2 * t * lanes : 2 * (t + 1) * lanes]
                    outs[t][here, cols] = (z * scale if t == 0 else z).astype(BF16)
                return 0

            lax.fori_loop(0, 3, project, 0)

        for c in early_out(g):
            c.start()

        def run(it, _):
            attend(it, g)
            return 0

        lax.fori_loop(0, TILE // 4, run, 0)

        @pl.when(g == 0)
        def _():
            for r in evens:
                if r >= twice:
                    main.forward(r)

        @pl.when(g == groups - 1)
        def _():
            for r in evens:
                rest.forward(r)

        lax.fori_loop(TILE // 4, TILE // 2, run, 0)
        for c in late_out(g):
            c.start()

        @pl.when(g == groups - 1)
        def _():
            main.straight(1).wait_send()
            for r in evens:
                main.straight(r).wait_send()
                main.onward(r).wait_send()
            rest.finish()
            for known in range(groups):
                for c in early_out(known) + late_out(known):
                    c.wait()


def front_rows(
    x, g0, b0, wm, g1, b1, qkvw, qkvb, tab, ub, up, down, proj, idx, rid, size, head_dim
):
    rows, wide = x.shape
    width = wm.shape[1]
    local = qkvb.shape[0]
    hidden = up.shape[1]
    heads = width // head_dim
    groups = heads // GROUP
    offsets, sets = rid.shape[0], rid.shape[1]
    cover = GROUP * COVER
    merge_steps = 7
    step = rows // merge_steps
    first = (3 * local * head_dim, width)
    second = (2 * hidden + local * head_dim, width)

    def place(i):
        return (jnp.minimum(i, merge_steps - 1), 0)

    def group_place(i):
        return (jnp.maximum(i - merge_steps, 0), 0, 0, 0, 0)

    small = [g0, b0, wm, g1, b1, qkvw, qkvb, tab, ub, up, down, proj, idx, rid]
    row_out = jax.ShapeDtypeStruct((rows, width), BF16)
    sems = [pltpu.SemaphoreType.DMA((size,))] * 6
    return call(
        functools.partial(front_kernel, head_dim, local, size, merge_steps),
        merge_steps + groups,
        [x] + small,
        [pl.BlockSpec((step, wide), place)] + [whole(a.shape) for a in small],
        [jax.ShapeDtypeStruct((rows, 8), F32), row_out]
        + [row_out] * 5
        + [
            jax.ShapeDtypeStruct((groups, offsets, sets, COVER, cover), BF16),
            jax.ShapeDtypeStruct((size, TILE, width), BF16),
            jax.ShapeDtypeStruct((3 * width, width), BF16),
            jax.ShapeDtypeStruct((size,) + second, BF16),
        ],
        [pl.BlockSpec((step, 8), place), pl.BlockSpec((step, width), place)]
        + [anywhere()] * 5
        + [
            pl.BlockSpec((1, offsets, sets, COVER, cover), group_place),
            whole((size, TILE, width)),
            whole((3 * width, width)),
            anywhere(),
        ],
        [
            pltpu.VMEM((size,) + first, BF16),
            pltpu.VMEM((size, TILE, width), BF16),
            pltpu.VMEM(first, BF16),
            pltpu.VMEM((TILE, width), BF16),
            pltpu.VMEM(second, BF16),
        ]
        + [pltpu.VMEM((rows, width), BF16)] * 6
        + [
            pltpu.VMEM((heads, COVER, COVER), F32),
            pltpu.VMEM((groups, TILE, COVER, cover), F32),
            pltpu.VMEM((cover, GROUP * head_dim), BF16),
        ]
        + sems
        + [pltpu.SemaphoreType.DMA((2,)), pltpu.SemaphoreType.DMA((5, groups))],
        2 * rows * width * (wide + 18 * width),
        rows * width * 40,
        group=0,
    )


REACH = math.sqrt(2.0) / 0.3275911
CENTRE = 0.125


def centred():
    rational = (0.254829592, -0.284496736, 1.421413741, -1.453152027, 1.061405429)
    plain = [0.5 * a * REACH ** (k + 1) for k, a in enumerate(rational)]
    out = [0.0] * len(plain)
    for k, a in enumerate(plain):
        for j in range(k + 1):
            out[j] += a * math.comb(k, j) * CENTRE ** (k - j)
    return out


def gelu_and_slope(pre):
    x = pre.astype(BF16)
    t = pl.reciprocal(jnp.abs(pre) + REACH, approx=True)
    s = (t - CENTRE).astype(BF16)
    terms = [BF16(a) for a in centred()]
    poly = terms[4]
    for a in reversed(terms[:4]):
        poly = poly * s + a
    part = poly * t.astype(BF16)
    bell = jnp.exp2((x * x) * BF16(-0.5 * math.log2(math.e)))
    size = jnp.abs(x)
    act = jnp.maximum(x, BF16(0.0)) - size * (part * bell)
    under = (part - size * BF16(1.0 / math.sqrt(2.0 * math.pi))) * bell
    return act, jnp.where(x > BF16(0.0), BF16(1.0) - under, under)


def live_rows(live_ref, start, count, rows, width, window):
    micro = live_ref.shape[0]
    micro_rows = rows // micro
    before = lax.axis_index("mp") * micro_rows
    row = lax.broadcasted_iota(jnp.int32, (count, width), 0) + start
    live = None
    for m in range(micro):
        last = m * micro_rows + jnp.minimum(live_ref[m, 0] * window - before, micro_rows)
        inside = (row >= m * micro_rows) & (row < last)
        live = inside if live is None else live | inside
    return live


def ffn_kernel(
    local,
    window,
    live_ref,
    n1_ref,
    att_ref,
    cot_ref,
    stats_ref,
    wp_ref,
    pb_ref,
    g2_ref,
    b2_ref,
    db_ref,
    tail_ref,
    up_ref,
    down_ref,
    base_ref,
    act_ref,
    gmid_ref,
    gatt_ref,
    part_ref,
    gub_ref,
    gproj_ref,
    sums_ref,
    base_s,
    gffn_s,
    att_s,
    n2_s,
    inv_s,
    n_s,
    go_s,
    nt_s,
    gt_s,
    act_s,
    gp_s,
    odd_s,
    even_s,
    near_s,
    far_s,
    near_send,
    near_recv,
    far_send,
    far_recv,
    in_sems,
    out_sems,
    act_sem,
):
    step = pl.program_id(0)
    pairs = even_s.shape[0]
    pair = pairs - 1 - step
    rows, width = gffn_s.shape
    blocks = spans(rows, 384)
    hidden = up_ref.shape[1]
    wp = wp_ref[...].reshape(width, width)

    def near(p):
        return send("mp", 1, odd_s.at[p % 2], near_s.at[p], near_send.at[p], near_recv.at[p])

    def far(p):
        slot = far_s.at[p - 1]
        return send("mp", 2 * p, even_s.at[p], slot, far_send.at[p], far_recv.at[p])

    def bring(b):
        here = pl.ds(*blocks[b])
        whence = ((n1_ref, n_s), (att_ref, att_s), (cot_ref, go_s))
        return [
            pltpu.make_async_copy(src.at[here], dst.at[here], in_sems.at[i, b])
            for i, (src, dst) in enumerate(whence)
        ]

    def take(which, b):
        here = pl.ds(*blocks[b])
        src, dst = ((base_s, base_ref), (go_s, gmid_ref), (n2_s, gatt_ref))[which]
        return pltpu.make_async_copy(src.at[here], dst.at[here], out_sems.at[which, b])

    def take_act():
        return pltpu.make_async_copy(act_s.at[pl.ds(0, rows)], act_ref.at[pair], act_sem)

    @pl.when(step == 0)
    def _():
        for b in range(len(blocks)):
            for c in bring(b):
                c.start()
        greet([("mp", r) for r in [1] + [2 * p for p in range(1, pairs)]])
        bias_proj, gain2, bias2, bias_down = (x[...] for x in (pb_ref, g2_ref, b2_ref, db_ref))
        act_s[rows:, :] = jnp.zeros_like(act_s[rows:, :])
        gp_s[rows:, :] = jnp.zeros_like(gp_s[rows:, :])
        nt_s[width:, :] = jnp.ones_like(nt_s[width:, :])
        down_sum = jnp.zeros((1, width), F32)
        for b, (start, count) in enumerate(blocks):
            here = pl.ds(start, count)
            for c in bring(b):
                c.wait()
            stats = stats_ref[here, :]
            merged = n_s[here, :].astype(F32) * stats[:, 4:5] + stats[:, 2:3]
            middle = merged + dot(att_s[here, :], wp) + bias_proj
            base_s[here, :] = (middle + bias_down).astype(BF16)
            take(0, b).start()
            normed, _, inverse, _ = norm_parts(middle)
            n2_s[here, :] = normed.astype(BF16)
            inv_s[here, :] = jnp.broadcast_to(inverse, (count, inv_s.shape[1]))
            normed_ffn = (normed * gain2 + bias2).astype(BF16)
            n_s[here, :] = normed_ffn
            live = live_rows(live_ref, start, count, rows, width, window)
            grad_out = jnp.where(live, go_s[here, :].astype(F32), 0.0)
            down_sum = down_sum + jnp.sum(grad_out, axis=0, keepdims=True)
            grad_low = grad_out.astype(BF16)
            go_s[here, :] = grad_low
            whole_count = -(-count // 128) * 128
            if whole_count != count:
                filler = jnp.zeros((whole_count - count, width), BF16)
                normed_ffn = jnp.concatenate([normed_ffn, filler], axis=0)
                grad_low = jnp.concatenate([grad_low, filler], axis=0)
            nt_s[:width, start : start + whole_count] = normed_ffn.T
            gt_s[:, start : start + whole_count] = grad_low.T
        sums_ref[...] = jnp.zeros_like(sums_ref)
        sums_ref[3:4, :] = down_sum
        gffn_s[...] = jnp.zeros_like(gffn_s)

    def pass_on():
        @pl.when(step > 0)
        def _():
            near(pair + 1).wait_recv()
            joined = even_s[pair + 1].astype(F32) + near_s[pair + 1].astype(F32)
            even_s[pair + 1] = joined.astype(BF16)

        for p in range(1, pairs):

            @pl.when(pair + 1 == p)
            def _():
                far(p).start()

    up_t = up_ref[...].reshape(2 * hidden, width)
    down = down_ref[...].reshape(2 * hidden, width)
    up_bias = jnp.concatenate(
        [tail_ref[i].astype(F32)[3 + local : 4 + local, :hidden] for i in range(2)], axis=1
    )
    for b, (start, count) in enumerate(blocks):
        if b == 1:
            pass_on()
        here = pl.ds(start, count)
        act, slope = gelu_and_slope(dot_rt(n_s[here, :], up_t) + up_bias)
        grad_pre = dot_rt(go_s[here, :], down).astype(BF16) * slope
        act_s[here, :] = act
        gp_s[here, :] = grad_pre
        gffn_s[here, :] += dot(grad_pre, up_t)
    take_act().start()

    @pl.when(step > 1)
    def _():
        near(pair + 2).wait_send()

    grad_up = dot(nt_s[...], gp_s[...])
    gub_ref[0] = grad_up[width : width + 1, :]
    grad_up = grad_up[:width].astype(BF16)
    even_s[pair, :, :hidden] = grad_up[:, :hidden]
    odd_s[pair % 2, :, :hidden] = grad_up[:, hidden:]
    grad_down = dot(gt_s[...], act_s[...]).astype(BF16)
    even_s[pair, :, hidden:] = grad_down[:, :hidden]
    odd_s[pair % 2, :, hidden:] = grad_down[:, hidden:]
    near(pair).start()
    take_act().wait()

    @pl.when(step == pairs - 1)
    def _():
        gain2 = g2_ref[...]
        gain_sum = jnp.zeros((1, width), F32)
        bias_sum = jnp.zeros((1, width), F32)
        proj_sum = jnp.zeros((1, width), F32)
        grad_proj = jnp.zeros((width, width), F32)
        for b, (start, count) in enumerate(blocks):
            here = pl.ds(start, count)
            grad_ffn = gffn_s[here, :]
            normed = n2_s[here, :].astype(F32)
            gain_sum = gain_sum + jnp.sum(grad_ffn * normed, axis=0, keepdims=True)
            bias_sum = bias_sum + jnp.sum(grad_ffn, axis=0, keepdims=True)
            grad_middle = go_s[here, :].astype(F32) + norm_back(
                grad_ffn * gain2, normed, inv_s[here, :1]
            )
            proj_sum = proj_sum + jnp.sum(grad_middle, axis=0, keepdims=True)
            grad_attn = grad_middle.astype(BF16)
            go_s[here, :] = grad_attn
            take(1, b).start()
            grad_proj = grad_proj + dot_lt(att_s[here, :], grad_attn)
            n2_s[here, :] = dot_rt(grad_attn, wp).astype(BF16)
            take(2, b).start()
        gproj_ref[...] = grad_proj.astype(BF16)
        sums_ref[0:1, :] = proj_sum
        sums_ref[1:2, :] = gain_sum
        sums_ref[2:3, :] = bias_sum
        near(0).wait_recv()
        total = even_s[0].astype(F32) + near_s[0].astype(F32)
        for p in range(1, pairs):
            far(p).wait_recv()
            total = total + far_s[p - 1].astype(F32)
        part_ref[...] = total.astype(BF16)
        for p in range(pairs):
            if p < 2:
                near(p).wait_send()
            if p:
                far(p).wait_send()
        for b in range(len(blocks)):
            for which in range(3):
                take(which, b).wait()


def ffn_rows(live, n1, att, cot, stats, tiles, second, vecs, local, hidden, window):
    rows, width = n1.shape
    size = tiles.shape[0]
    pairs = size // 2
    padded = -(-rows // 128) * 128
    proj_rows = width // size
    proj_at = 2 * hidden // proj_rows
    blocks = len(spans(rows, 384))
    row_out = jax.ShapeDtypeStruct((rows, width), BF16)
    return call(
        functools.partial(ffn_kernel, local, window),
        pairs,
        (live, n1, att, cot, stats, second) + vecs + (tiles, second, second),
        [
            pl.BlockSpec(memory_space=pltpu.SMEM),
            anywhere(),
            anywhere(),
            anywhere(),
            whole(stats.shape),
            pl.BlockSpec(
                (size, proj_rows, width),
                lambda i: (0, proj_at, 0),
                pipeline_mode=pl.Buffered(1),
            ),
        ]
        + [whole((1, width))] * 4
        + [
            pl.BlockSpec((2, TILE, width), lambda i: (pairs - 1 - i, 0, 0)),
            pl.BlockSpec((2, hidden, width), lambda i: (pairs - 1 - i, 0, 0)),
            pl.BlockSpec((2, hidden, width), lambda i: (pairs - 1 - i, 1, 0)),
        ],
        [
            row_out,
            jax.ShapeDtypeStruct((pairs, rows, 2 * hidden), BF16),
            row_out,
            row_out,
            jax.ShapeDtypeStruct((width, 2 * hidden), BF16),
            jax.ShapeDtypeStruct((pairs, 1, 2 * hidden), F32),
            jax.ShapeDtypeStruct((width, width), BF16),
            jax.ShapeDtypeStruct((8, width), F32),
        ],
        [
            anywhere(),
            anywhere(),
            anywhere(),
            anywhere(),
            whole((width, 2 * hidden)),
            pl.BlockSpec((1, 1, 2 * hidden), lambda i: (pairs - 1 - i, 0, 0)),
            whole((width, width)),
            whole((8, width)),
        ],
        [
            pltpu.VMEM((rows, width), BF16),
            pltpu.VMEM((rows, width), F32),
            pltpu.VMEM((rows, width), BF16),
            pltpu.VMEM((rows, width), BF16),
            pltpu.VMEM((rows, 128), F32),
            pltpu.VMEM((rows, width), BF16),
            pltpu.VMEM((rows, width), BF16),
            pltpu.VMEM((width + TILE, padded), BF16),
            pltpu.VMEM((width, padded), BF16),
            pltpu.VMEM((padded, 2 * hidden), BF16),
            pltpu.VMEM((padded, 2 * hidden), BF16),
        ]
        + [pltpu.VMEM((min(pairs, 2), width, 2 * hidden), BF16)]
        + [pltpu.VMEM((pairs, width, 2 * hidden), BF16)] * 2
        + [pltpu.VMEM((max(pairs - 1, 1), width, 2 * hidden), BF16)]
        + [pltpu.SemaphoreType.DMA((pairs,))] * 4
        + [pltpu.SemaphoreType.DMA((3, blocks))] * 2
        + [pltpu.SemaphoreType.DMA(())],
        2 * rows * width * hidden * size * 6,
        rows * width * 20,
        group=1,
    )


LEVELS = 4
PARTS = 3


def back_kernel(
    head_dim,
    local,
    near_size,
    far_size,
    dense_steps,
    q_ref,
    k_ref,
    v_ref,
    ga_ref,
    rinv_ref,
    att_ref,
    n1_ref,
    wt_ref,
    p_ref,
    idx_ref,
    ffn_ref,
    gmid_ref,
    stats_ref,
    x_ref,
    g1_ref,
    b1_ref,
    gproj_ref,
    gub_ref,
    sums2_ref,
    act_ref,
    base_ref,
    second_ref,
    wm_ref,
    g0_ref,
    raw_ref,
    gin_ref,
    ffnsum_ref,
    main_ref,
    tail_ref,
    full_ref,
    sums_ref,
    q_s,
    k_s,
    v_s,
    ga_s,
    rinv_s,
    att_s,
    n1_s,
    wt_s,
    gq_s,
    gk_s,
    gv_s,
    ds_s,
    base_s,
    mask_s,
    gtab_s,
    ffncame_s,
    ffnown_s,
    merge_s,
    merged_s,
    mnear_s,
    mfar_s,
    mpiece_s,
    tparts_s,
    tnear_s,
    tfar_s,
    parts_s,
    pnear_s,
    pfar_s,
    main_s,
    mainsum_s,
    tails_s,
    linein_s,
    lineout_s,
    lines_s,
    n0_s,
    inv0_s,
    wm_s,
    down_s,
    in_sems,
    more_sems,
    late_sems,
    out_sems,
    sems,
):
    step = pl.program_id(0)
    rows, width = gq_s.shape
    lanes = GROUP * head_dim
    groups = width // lanes
    scale = 1.0 / math.sqrt(head_dim)
    sets = p_ref.shape[2]
    block = rows // sets
    jump = block // TILE - 1
    pairs = near_size // 2
    span = local * head_dim
    me, deep = lax.axis_index("mp"), lax.axis_index("dp")
    beside = list(range(1, near_size))
    behind = list(range(1, far_size))
    evens = list(range(2, near_size, 2))
    piece = ffnsum_ref.shape[1]
    at_sem = [0]

    def copy(axis, r, src, dst):
        at_sem[0] += 2
        return send(axis, r, src, dst, sems.at[at_sem[0] - 2], sems.at[at_sem[0] - 1])

    def rows_at(ref, index, count):
        return ref.at[pl.ds(pl.multiple_of(index * count, TILE), count)]

    def bring(level):
        copies = []
        whence = (
            (q_ref, q_s),
            (k_ref, k_s),
            (v_ref, v_s),
            (ga_ref, ga_s),
            (rinv_ref, rinv_s),
            (att_ref, att_s),
        )
        part = TILE // LEVELS * jump
        first = COVER - jump
        for i, (src, dst) in enumerate(whence):
            for u in range(sets):
                if level == 0:
                    here = pl.ds(u * block, part + first)
                else:
                    here = pl.ds(u * block + first + level * part, part)
                copies.append(
                    pltpu.make_async_copy(src.at[here], dst.at[here], in_sems.at[i, level, u])
                )
        return copies

    def bring_more():
        return [
            pltpu.make_async_copy(n1_ref, n1_s, more_sems.at[0]),
            pltpu.make_async_copy(wt_ref, wt_s, more_sems.at[1]),
        ]

    act_bufs = (k_s, v_s, ga_s, rinv_s)
    chunks = act_ref.shape[0] * act_ref.shape[2] // width

    def bring_late():
        copies = [(base_ref, att_s), (wm_ref, wm_s)]
        per = act_ref.shape[2]
        each = width // per
        for p in range(act_ref.shape[0]):
            dst = act_bufs[p // each].at[:, pl.ds(p % each * per, per)]
            copies.append((act_ref.at[p], dst))
        hidden = per // 2
        for r in range(near_size):
            src = second_ref.at[r, pl.ds(hidden, hidden)]
            copies.append((src, down_s.at[pl.ds(r * hidden, hidden)]))
        return [
            pltpu.make_async_copy(src, dst, late_sems.at[i]) for i, (src, dst) in enumerate(copies)
        ]

    def dense_span(j):
        return pl.ds(j * (rows // PARTS), rows // PARTS)

    def take_gin(j):
        here = dense_span(j)
        return pltpu.make_async_copy(n0_s.at[here], gin_ref.at[here], out_sems.at[0, j])

    def take_raw(j):
        here = dense_span(j)
        return pltpu.make_async_copy(att_s.at[here], raw_ref.at[here], out_sems.at[1, j])

    def input_part(j):
        here = dense_span(j)
        grad_low = dot_rt(q_s[here, :], wm_s[...])
        normed = n0_s[here, :].astype(F32)
        grad = norm_back(grad_low * g0_ref[...], normed, inv0_s[here, :1])
        n0_s[here, :] = grad.astype(BF16)
        take_gin(j).start()

    def output_part(j):
        here = dense_span(j)
        total = att_s[here, :].astype(F32)
        for i in range(chunks):
            total = total + dot(act_bufs[i][here, :], down_s[i * width : (i + 1) * width, :])
        att_s[here, :] = total.astype(BF16)
        take_raw(j).start()

    def keep_main():
        return pltpu.make_async_copy(mainsum_s, main_ref.at[deep], more_sems.at[3])

    def keep_merge(h):
        src = mpiece_s.at[h, 0]
        return pltpu.make_async_copy(src, full_ref.at[h, me, deep], more_sems.at[4 + h])

    def keep_ffn():
        return pltpu.make_async_copy(ffnown_s, ffnsum_ref.at[deep], more_sems.at[2])

    ffn_out = [
        copy("dp", r, rows_at(ffn_ref, partner("dp", r), piece), ffncame_s.at[r]) for r in behind
    ]
    ffn_all = [copy("dp", r, ffnown_s, ffnsum_ref.at[deep]) for r in behind]

    halves = mfar_s.shape[0]
    half_rows = merged_s.shape[0] // halves
    share = half_rows // near_size
    small = share // far_size
    main_piece = parts_s.shape[1] // far_size

    def share_at(h, index):
        return h * half_rows + index * share

    def share_of(h, index):
        return merged_s.at[pl.ds(pl.multiple_of(share_at(h, index), TILE), share)]

    mnear, mfar, across, back, spread, onward = [], [], [], [], [], []
    for h in range(halves):
        mnear.append([])
        for p in range(pairs):
            src = share_of(h, partner("mp", 2 * p + 1))
            mnear[h].append(copy("mp", 1, src, mnear_s.at[h, p]))
        mfar.append({})
        for p in range(1, pairs):
            src = share_of(h, partner("mp", 2 * p))
            mfar[h][p] = copy("mp", 2 * p, src, mfar_s.at[h, p])
        across.append([])
        for r in behind:
            src = rows_at(mfar_s.at[h, 0], partner("dp", r), small)
            across[h].append(copy("dp", r, src, mpiece_s.at[h, r]))
        mine = full_ref.at[h, me]
        back.append([copy("dp", r, mpiece_s.at[h, 0], mine.at[deep]) for r in behind])
        spread.append([copy("mp", r, mine, mine) for r in evens + [1]])
        onward.append([])
        for r in evens:
            came = full_ref.at[h, partner("mp", r)]
            onward[h].append(copy("mp", 1, came, came))
    lines_in = [copy("mp", r, linein_s.at[0], linein_s.at[r]) for r in beside]
    lines_out = [copy("dp", r, lineout_s.at[0], lineout_s.at[r]) for r in behind]
    pnear = [copy("mp", 1, parts_s.at[2 * p + 1], pnear_s.at[p]) for p in range(pairs)]
    pfar = {p: copy("mp", 2 * p, parts_s.at[2 * p], pfar_s.at[p]) for p in range(1, pairs)}
    main_out = [
        copy("dp", r, rows_at(parts_s.at[0], partner("dp", r), main_piece), main_s.at[r])
        for r in behind
    ]
    main_all = [copy("dp", r, mainsum_s, main_ref.at[deep]) for r in behind]
    tnear = [copy("mp", 1, tparts_s.at[2 * p + 1], tnear_s.at[p]) for p in range(pairs)]
    tfar = {p: copy("mp", 2 * p, tparts_s.at[2 * p], tfar_s.at[p]) for p in range(1, pairs)}
    tails = [copy("dp", r, tparts_s.at[0], tails_s.at[r]) for r in behind]

    @pl.when(step == 0)
    def _():
        for level in range(LEVELS):
            for c in bring(level):
                c.start()
        for c in bring_more():
            c.start()
        greet([("mp", r) for r in beside] + [("dp", r) for r in behind])
        for c in ffn_out:
            c.start()
        mask_s[...] = head_mask(head_dim)
        gq_s[...] = jnp.zeros_like(gq_s)
        gk_s[...] = jnp.zeros_like(gk_s)
        gv_s[...] = jnp.zeros_like(gv_s)

    @pl.when(step == TILE // 2)
    def _():
        total = ffn_ref[pl.ds(pl.multiple_of(deep * piece, TILE), piece), :].astype(F32)
        for c, r in zip(ffn_out, behind):
            c.wait_recv()
            total = total + ffncame_s[r].astype(F32)
        ffnown_s[...] = total.astype(BF16)
        keep_ffn().start()
        for c in ffn_all:
            c.start()

    for level in range(LEVELS):

        @pl.when(step == level * (TILE // LEVELS))
        def _():
            for c in bring(level):
                c.wait()

    @pl.when(step < TILE)
    def _():
        mask = mask_s[...]
        minus = -mask
        starts = [pl.multiple_of(step * jump + u * block, TILE) for u in range(sets)]
        lane_head = lax.broadcasted_iota(jnp.int32, (COVER, 2 * lanes), 1) % lanes // head_dim
        zeros = jnp.zeros((COVER, lanes), BF16)
        units = [(u, g) for g in range(groups) for u in range(sets)]

        def at(ref, u, g):
            return ref[pl.ds(starts[u], COVER), pl.ds(g * lanes, lanes)]

        scaled = [at(ga_s, u, g) * at(rinv_s, u, g) for u, g in units]
        grads = []
        for (u, g), ga in zip(units, scaled):
            left = jnp.concatenate([ga, ga * at(att_s, u, g)], axis=1)
            right = jnp.concatenate([tiled(at(v_s, u, g), mask), minus], axis=1)
            grads.append(dot_rt(left, right))
        score_grads = []
        totals = {}
        for (u, g), grad in zip(units, grads):
            ds = p_ref[g, 0, u].astype(F32) * grad
            totals[g] = ds if g not in totals else totals[g] + ds
            score_grads.append(ds.astype(BF16))
        for g in range(groups):
            ds_s[step, g] = totals[g]
        query_grads = []
        for (u, g), ds in zip(units, score_grads):
            query_grads.append(dot(ds, tiled(at(k_s, u, g), mask)))
        pair_grads = []
        for (u, g), ds, ga in zip(units, score_grads, scaled):
            left = jnp.concatenate([ds, p_ref[g, 0, u]], axis=0)
            right = jnp.concatenate(
                [
                    jnp.concatenate([at(q_s, u, g), zeros], axis=1),
                    jnp.concatenate([zeros, ga], axis=1),
                ],
                axis=0,
            )
            pair_grads.append(dot_lt(left, right))
        for (u, g), grad_q, grad_kv in zip(units, query_grads, pair_grads):
            here, cols = pl.ds(starts[u], COVER), pl.ds(g * lanes, lanes)
            gq_s[here, cols] += (grad_q * scale).astype(BF16)
            both = jnp.where(lane_head == 0, grad_kv[:COVER], 0.0)
            for h in range(1, GROUP):
                both = jnp.where(lane_head == h, grad_kv[h * COVER : (h + 1) * COVER], both)
            both = both.astype(BF16)
            gk_s[here, cols] += both[:, :lanes]
            gv_s[here, cols] += both[:, lanes:]

    def table_grads():
        def unshift(g, _):
            full = ds_s[0, g]
            for o in range(1, TILE):
                turned = pltpu.roll(ds_s[o, g], COVER - o, 0)
                full = full + pltpu.roll(turned, GROUP * COVER - o, 1)
            for h in range(GROUP):
                base_s[g * GROUP + h] = full[:, h * COVER : (h + 1) * COVER]
            return 0

        lax.fori_loop(0, groups, unshift, 0)
        sums = []
        for pair in range((idx_ref.shape[0] + 1) // 2):
            onehot = index_onehot(pair_row(idx_ref, pair), gtab_s.shape[1])
            vals = jnp.concatenate([base_s[:, 2 * pair, :], base_s[:, 2 * pair + 1, :]], axis=1)
            high = vals.astype(BF16)
            both = jnp.concatenate([high, (vals - high.astype(F32)).astype(BF16)], axis=0)
            sums.append(dot_rt(both, onehot))
        count = base_s.shape[0]
        grad = sums[0]
        for x in sums[1:]:
            grad = grad + x
        gtab_s[...] = grad[:count] + grad[count:]

    @pl.when(step == TILE)
    def _():
        for c in bring_late():
            c.start()
        merge_s[...] = jnp.zeros_like(merge_s)
        lines_s[...] = jnp.zeros_like(lines_s)
        for c in bring_more():
            c.wait()
        normed_t = n1_s[...].T
        for t, ref in enumerate((gq_s, gk_s, gv_s)):
            grad = dot(normed_t, ref[...]).T
            sums = jnp.sum(ref[...].astype(F32), axis=0, keepdims=True)
            lines_s[4 + t : 5 + t, :] = sums
            sums = jnp.broadcast_to(sums, (8, width)).T[:, :1]
            grad = (grad * g1_ref[...] + sums * b1_ref[...]).astype(BF16)
            for r in range(near_size):
                parts_s[r, t * span : (t + 1) * span, :] = grad[r * span : (r + 1) * span]
        for r in range(near_size):
            parts_s[r, 3 * span :, :] = gproj_ref[r * span : (r + 1) * span, :]
        for c in pnear:
            c.start()

    @pl.when(step == TILE + 2)
    def _():
        for p in reversed(range(pairs)):
            pnear[p].wait_recv()
            joined = parts_s[2 * p].astype(F32) + pnear_s[p].astype(F32)
            parts_s[2 * p] = joined.astype(BF16)
            if p:
                pfar[p].start()

    @pl.when(step >= TILE)
    def _():
        count = gmid_ref.shape[0]
        here = pl.ds(pl.multiple_of((step - TILE) * count, TILE), count)
        grad_mid = None
        for t, ref in enumerate((gq_s, gk_s, gv_s)):
            part = dot(ref[here, :], wt_s[t * width : (t + 1) * width, :])
            grad_mid = part if grad_mid is None else grad_mid + part
        stats = stats_ref[...]
        normed1 = n1_s[here, :].astype(F32)
        lines_s[0:1, :] += jnp.sum(grad_mid * normed1, axis=0, keepdims=True)
        lines_s[1:2, :] += jnp.sum(grad_mid, axis=0, keepdims=True)
        grad_merged = gmid_ref[...].astype(F32) + norm_back(
            grad_mid * g1_ref[...], normed1, stats[:, 3:4]
        )
        lines_s[2:3, :] += jnp.sum(grad_merged, axis=0, keepdims=True)
        grad_merged = grad_merged.astype(BF16)
        q_s[here, :] = grad_merged
        normed0 = ((x_ref[...].astype(F32) - stats[:, 0:1]) * stats[:, 1:2]).astype(BF16)
        n0_s[here, :] = normed0
        inv0_s[here, :] = jnp.broadcast_to(stats[:, 1:2], (count, inv0_s.shape[1]))
        merge_s[...] += dot_lt(grad_merged, normed0)

    @pl.when(step == TILE + dense_steps - 1)
    def _():
        narrow = merged_s.shape[1]
        per_half = merge_s.shape[1] // narrow // halves
        for h in range(halves):
            for j in range(h * per_half, (h + 1) * per_half):
                part = merge_s[:, j * narrow : (j + 1) * narrow]
                merged_s[j * width : (j + 1) * width, :] = part.astype(BF16)
            for c in mnear[h]:
                c.start()
        linein_s[0] = jnp.concatenate([sums2_ref[0:4, :], lines_s[0:4, :]], axis=0)
        for c in lines_in:
            c.start()
        for c in bring_late():
            c.wait()
        table_grads()
        for r in range(near_size):
            bias_sums = lines_s[4:7, r * span : (r + 1) * span]
            hidden = gub_ref.shape[2] // 2
            half = (r % 2) * hidden
            lines = [
                fill(bias_sums, width),
                fill(gtab_s[r * local : (r + 1) * local, :], width),
                fill(gub_ref[r // 2][:, half : half + hidden], width),
                jnp.zeros((TILE - 4 - local, width), F32),
            ]
            tparts_s[r] = jnp.concatenate(lines, axis=0).astype(BF16)
        for h in range(halves):
            for p in reversed(range(pairs)):
                mnear[h][p].wait_recv()
                spot = pl.ds(pl.multiple_of(share_at(h, partner("mp", 2 * p)), TILE), share)
                joined = merged_s[spot, :].astype(F32) + mnear_s[h, p].astype(F32)
                merged_s[spot, :] = joined.astype(BF16)
                if p:
                    mfar[h][p].start()
        for c in tnear:
            c.start()
        total = linein_s[0]
        for c, r in zip(lines_in, beside):
            c.wait_recv()
            total = total + linein_s[r]
        lineout_s[0] = total
        for c in lines_out:
            c.start()
        input_part(0)

        total = parts_s[0].astype(F32)
        for p in reversed(range(1, pairs)):
            pfar[p].wait_recv()
            total = total + pfar_s[p].astype(F32)
        parts_s[0] = total.astype(BF16)
        for c in main_out:
            c.start()
        for h in range(halves):
            mine = pl.ds(pl.multiple_of(share_at(h, me), TILE), share)
            total = merged_s[mine, :].astype(F32)
            for p in reversed(range(1, pairs)):
                mfar[h][p].wait_recv()
                total = total + mfar_s[h, p].astype(F32)
            mfar_s[h, 0] = total.astype(BF16)
            for c in across[h]:
                c.start()
        for p in reversed(range(pairs)):
            tnear[p].wait_recv()
            tparts_s[2 * p] = (tparts_s[2 * p].astype(F32) + tnear_s[p].astype(F32)).astype(BF16)
            if p:
                tfar[p].start()
        input_part(1)

        for h in range(halves):
            spot = pl.ds(pl.multiple_of(deep * small, TILE), small)
            total = mfar_s[h, 0, spot, :].astype(F32)
            for c, r in zip(across[h], behind):
                c.wait_recv()
                total = total + mpiece_s[h, r].astype(F32)
            mpiece_s[h, 0] = total.astype(BF16)
            keep_merge(h).start()
            for c in back[h]:
                c.start()
        spot = pl.ds(pl.multiple_of(deep * main_piece, TILE), main_piece)
        total = parts_s[0, spot, :].astype(F32)
        for c, r in zip(main_out, behind):
            c.wait_recv()
            total = total + main_s[r].astype(F32)
        mainsum_s[...] = total.astype(BF16)
        keep_main().start()
        for c in main_all:
            c.start()
        input_part(2)

        for h in range(halves):
            keep_merge(h).wait()
            for c in back[h]:
                c.wait_recv()
            for c in spread[h]:
                c.start()
        total = tparts_s[0].astype(F32)
        for p in reversed(range(1, pairs)):
            tfar[p].wait_recv()
            total = total + tfar_s[p].astype(F32)
        tparts_s[0] = total.astype(BF16)
        for c in tails:
            c.start()
        output_part(0)
        output_part(1)
        for h in range(halves):
            for c, after in zip(spread[h], onward[h]):
                c.wait_recv()
                after.start()
            if h == 0:
                output_part(2)

        total = lineout_s[0]
        for c, r in zip(lines_out, behind):
            c.wait_recv()
            total = total + lineout_s[r]
        sums_ref[...] = total
        total = tparts_s[0].astype(F32)
        for c, r in zip(tails, behind):
            c.wait_recv()
            total = total + tails_s[r].astype(F32)
        tail_ref[...] = total
        for h in range(halves):
            spread[h][-1].wait_recv()
            for c in onward[h]:
                c.wait_recv()
        for c in main_all + ffn_all:
            c.wait_recv()
        keep_ffn().wait()
        keep_main().wait()
        for h in range(halves):
            for c in mnear[h] + list(mfar[h].values()) + across[h] + back[h] + spread[h]:
                c.wait_send()
            for c in onward[h]:
                c.wait_send()
        for c in ffn_out + ffn_all + lines_in + lines_out + tnear + list(tfar.values()):
            c.wait_send()
        for c in pnear + list(pfar.values()) + main_out + tails + main_all:
            c.wait_send()
        for j in range(PARTS):
            take_gin(j).wait()
            take_raw(j).wait()


def back_rows(
    q,
    k,
    v,
    ga,
    rinv,
    att,
    n1,
    wt,
    p,
    idx,
    ffn,
    gmid,
    stats,
    x,
    g1,
    b1,
    gproj,
    gub,
    sums2,
    act,
    base,
    second,
    wm,
    g0,
    table_width,
    head_dim,
    local,
    near_size,
    far_size,
):
    rows, width = q.shape
    wide = x.shape[1]
    heads = width // head_dim
    groups, steps, sets, _, cover = p.shape
    dense_steps = 7
    count = rows // dense_steps
    narrow = 256
    pairs = near_size // 2
    piece = (ffn.shape[0] // far_size, ffn.shape[1])
    part = (4 * local * head_dim, width)
    main_piece = (4 * local * head_dim // far_size, width)
    total_rows = wide // narrow * width
    halves = 2 if total_rows // (2 * near_size * far_size) % TILE == 0 else 1
    share = total_rows // halves // near_size
    small = share // far_size
    near, far = near_size - 1, far_size - 1
    copies = 2 * far + halves * (4 * pairs - 2 + 2 * far) + near + far
    copies += (2 * pairs - 1) + 2 * far + (2 * pairs - 1) + far

    def place(i):
        return (jnp.maximum(i - steps, 0), 0)

    def p_place(i):
        return (0, jnp.minimum(i, steps - 1), 0, 0, 0)

    return call(
        functools.partial(back_kernel, head_dim, local, near_size, far_size, dense_steps),
        steps + dense_steps,
        (q, k, v, ga, rinv, att, n1, wt, p, idx, ffn, gmid, stats, x, g1, b1, gproj, gub, sums2)
        + (act, base, second, wm, g0),
        [anywhere()] * 8
        + [
            pl.BlockSpec((groups, 1, sets, COVER, cover), p_place),
            whole(idx.shape),
            whole(ffn.shape),
            pl.BlockSpec((count, width), place),
            pl.BlockSpec((count, 8), place),
            pl.BlockSpec((count, wide), place),
            whole(g1.shape),
            whole(b1.shape),
            whole(gproj.shape),
            whole(gub.shape),
            whole(sums2.shape),
        ]
        + [anywhere()] * 4
        + [whole(g0.shape)],
        [
            jax.ShapeDtypeStruct((rows, width), BF16),
            jax.ShapeDtypeStruct((rows, wide), BF16),
            jax.ShapeDtypeStruct((far_size,) + piece, BF16),
            jax.ShapeDtypeStruct((far_size,) + main_piece, BF16),
            jax.ShapeDtypeStruct((TILE, width), F32),
            jax.ShapeDtypeStruct((halves, near_size, far_size, small, narrow), BF16),
            jax.ShapeDtypeStruct((8, width), F32),
        ],
        [
            anywhere(),
            anywhere(),
            anywhere(),
            anywhere(),
            whole((TILE, width)),
            anywhere(),
            whole((8, width)),
        ],
        [pltpu.VMEM((rows, width), BF16)] * 7
        + [pltpu.VMEM((3 * width, width), BF16)]
        + [pltpu.VMEM((rows, width), BF16)] * 3
        + [
            pltpu.VMEM((TILE, groups, COVER, cover), F32),
            pltpu.VMEM((heads, COVER, COVER), F32),
            pltpu.VMEM((cover, GROUP * head_dim), BF16),
            pltpu.VMEM((heads, table_width), F32),
            pltpu.VMEM((far_size,) + piece, BF16),
            pltpu.VMEM(piece, BF16),
            pltpu.VMEM((width, wide), F32),
            pltpu.VMEM((total_rows, narrow), BF16),
            pltpu.VMEM((halves, pairs, share, narrow), BF16),
            pltpu.VMEM((halves, pairs, share, narrow), BF16),
            pltpu.VMEM((halves, far_size, small, narrow), BF16),
            pltpu.VMEM((near_size, TILE, width), BF16),
            pltpu.VMEM((pairs, TILE, width), BF16),
            pltpu.VMEM((pairs, TILE, width), BF16),
            pltpu.VMEM((near_size,) + part, BF16),
            pltpu.VMEM((pairs,) + part, BF16),
            pltpu.VMEM((pairs,) + part, BF16),
            pltpu.VMEM((far_size,) + main_piece, BF16),
            pltpu.VMEM(main_piece, BF16),
            pltpu.VMEM((far_size, TILE, width), BF16),
            pltpu.VMEM((near_size, 8, width), F32),
            pltpu.VMEM((far_size, 8, width), F32),
            pltpu.VMEM((8, width), F32),
            pltpu.VMEM((rows, wide), BF16),
            pltpu.VMEM((rows, 128), F32),
            pltpu.VMEM(wm.shape, BF16),
            pltpu.VMEM((act.shape[0] * act.shape[2], width), BF16),
            pltpu.SemaphoreType.DMA((6, LEVELS, sets)),
            pltpu.SemaphoreType.DMA((4 + halves,)),
            pltpu.SemaphoreType.DMA((2 + act.shape[0] + near_size,)),
            pltpu.SemaphoreType.DMA((2, PARTS)),
            pltpu.SemaphoreType.DMA((2 * copies,)),
        ],
        2 * rows * width * (24 * width + wide),
        rows * width * 20,
        group=2,
    )


def last_kernel(
    head_dim,
    local,
    window,
    live_ref,
    raw_ref,
    gin16_ref,
    wm_ref,
    g0_ref,
    b0_ref,
    main_ref,
    ffn_ref,
    full_ref,
    sums_ref,
    tail_ref,
    out_ref,
    gin_ref,
    gain0_ref,
    bias0_ref,
    gmerge_ref,
    gqkv_ref,
    gproj_ref,
    gup_ref,
    gdown_ref,
    gqb_ref,
    gtab_ref,
    gub_ref,
    *line_refs,
):
    step = pl.program_id(0)
    count, width = raw_ref.shape
    rows = count * pl.num_programs(0)
    live = live_rows(live_ref, step * count, count, rows, width, window)
    out_ref[...] = jnp.where(live, raw_ref[...].astype(F32), 0.0)
    gin_ref[...] = gin16_ref[...].astype(F32)

    @pl.when(step == 0)
    def _():
        span = local * head_dim
        main = main_ref[...].astype(F32)
        order = [
            main[t * span + l * head_dim : t * span + (l + 1) * head_dim]
            for l in range(local)
            for t in range(3)
        ]
        grad = jnp.concatenate(order, axis=0).T
        for l in range(local):
            gqkv_ref[:, l, :] = grad[:, 3 * l * head_dim : 3 * (l + 1) * head_dim]
        gproj_ref[...] = main[3 * span :]
        rows_of = []
        for l in range(local):
            here = slice(l * head_dim, (l + 1) * head_dim)
            rows_of.append(
                jnp.concatenate([tail_ref[t : t + 1, here] for t in range(3)], axis=1)
            )
        gqb_ref[...] = jnp.concatenate(rows_of, axis=0)
        gtab_ref[...] = tail_ref[3 : 3 + local, : gtab_ref.shape[1]]
        gub_ref[...] = tail_ref[3 + local : 4 + local, : gub_ref.shape[1]]
        for i, ref in enumerate(line_refs):
            ref[...] = sums_ref[i : i + 1, :]

    @pl.when(step == 1)
    def _():
        hidden = gup_ref.shape[1]
        gup_ref[...] = ffn_ref[:, :hidden].astype(F32)
        gdown_ref[...] = ffn_ref[:, hidden:].astype(F32).T

    narrow = full_ref.shape[2]
    low_sum = sums_ref[6:7, :]
    for j in range(full_ref.shape[0]):

        @pl.when(step == 2 + j)
        def _():
            cols = pl.ds(j * narrow, narrow)
            grad = full_ref[j].astype(F32).T
            weight = wm_ref[cols, :].astype(F32)
            gain = jnp.sum(weight * grad, axis=1, keepdims=True)
            shift = jnp.sum(weight * low_sum, axis=1, keepdims=True)
            gain0_ref[:, cols] = jnp.broadcast_to(gain, (narrow, 128)).T[:1, :]
            bias0_ref[:, cols] = jnp.broadcast_to(shift, (narrow, 128)).T[:1, :]
            scale = jnp.broadcast_to(g0_ref[:, cols], (8, narrow)).T[:, :1]
            offset = jnp.broadcast_to(b0_ref[:, cols], (8, narrow)).T[:, :1]
            gmerge_ref[cols, :] = grad * scale + offset * low_sum


def last_rows(
    live, raw, gin16, wm, g0, b0, main, ffn, full, sums, tail, local, head_dim, rel, window
):
    rows, width = raw.shape
    wide = gin16.shape[1]
    step = rows // 7
    hidden = ffn.shape[1] // 2
    span = local * head_dim
    narrow_block = pl.BlockSpec((step, width), lambda i: (i, 0))
    wide_block = pl.BlockSpec((step, wide), lambda i: (i, 0))
    rest = [wm, g0, b0, main, ffn, full, sums, tail]
    shapes = [
        (1, wide),
        (1, wide),
        (wide, width),
        (width, local, 3 * head_dim),
        (span, width),
        (width, hidden),
        (hidden, width),
        (local, 3 * head_dim),
        (local, rel),
        (1, hidden),
    ] + [(1, width)] * 6
    return call(
        functools.partial(last_kernel, head_dim, local, window),
        7,
        [live, raw, gin16] + rest,
        [pl.BlockSpec(memory_space=pltpu.SMEM), narrow_block, wide_block]
        + [whole(a.shape) for a in rest],
        [
            jax.ShapeDtypeStruct((rows, width), F32),
            jax.ShapeDtypeStruct((rows, wide), F32),
        ]
        + [jax.ShapeDtypeStruct(shape, F32) for shape in shapes],
        [narrow_block, wide_block] + [whole(shape) for shape in shapes],
        [],
        2 * rows * width,
        rows * wide * 9,
    )


def shards(
    inputs,
    norm0_gain,
    norm0_bias,
    merge_weight,
    norm1_gain,
    norm1_bias,
    qkv_weight,
    qkv_bias,
    rel_table,
    rel_index,
    regions,
    live_windows,
    proj_weight,
    proj_bias,
    norm2_gain,
    norm2_bias,
    up_weight,
    up_bias,
    down_weight,
    down_bias,
    cotangent,
    n_dp,
    n_mp,
):
    micro, strip_rows, wide = inputs.shape
    width = merge_weight.shape[1]
    win = rel_index.shape[0]
    local, packed = qkv_bias.shape
    head_dim = packed // 3
    heads = local * n_mp
    hidden = up_bias.shape[0]
    rel = rel_table.shape[1]
    rows = micro * strip_rows
    windows = rows // win
    sets = windows // TILE
    strip = lax.axis_index("mp")

    region = lax.dynamic_slice_in_dim(regions, strip * strip_rows, strip_rows, axis=1)
    region = region.reshape(sets, rows // sets)
    jump = rows // sets // TILE - 1
    region = jnp.stack([region[:, o * jump : o * jump + COVER] for o in range(TILE)])
    region = jnp.tile(region[:, :, None, :], (1, 1, 1, GROUP))
    table_width = -(-rel // 128) * 128
    vecs = (proj_bias[None], norm2_gain[None], norm2_bias[None], down_bias[None])
    gain0, bias0 = norm0_gain[None], norm0_bias[None]
    gain1, bias1 = norm1_gain[None], norm1_bias[None]

    x = inputs.reshape(rows, wide)
    stats, n1, q, k, v, att, rinv, p, tiles, wt, second = front_rows(
        x,
        gain0,
        bias0,
        merge_weight,
        gain1,
        bias1,
        qkv_weight.reshape(width, local * packed),
        qkv_bias,
        rel_table,
        up_bias[None],
        up_weight,
        down_weight,
        proj_weight.reshape(local * head_dim, width),
        rel_index,
        region,
        n_mp,
        head_dim,
    )
    base, act, gmid, gatt, ffn_part, gub, gproj, sums2 = ffn_rows(
        live_windows,
        n1,
        att,
        cotangent.reshape(rows, width),
        stats,
        tiles,
        second,
        vecs,
        local,
        hidden,
        win,
    )
    raw, gin16, ffn_sum, main, tail, gmerge, sums = back_rows(
        q,
        k,
        v,
        gatt,
        rinv,
        att,
        n1,
        wt,
        p,
        rel_index,
        ffn_part,
        gmid,
        stats,
        x,
        gain1,
        bias1,
        gproj,
        gub,
        sums2,
        act,
        base,
        second,
        merge_weight,
        gain0,
        table_width,
        head_dim,
        local,
        n_mp,
        n_dp,
    )
    span = local * head_dim
    out, grad_input, ggain0, gbias0, gmerge, gqkv, gproj, gup, gdown, gqb, gtab, gub, *lines = (
        last_rows(
            live_windows,
            raw,
            gin16,
            merge_weight,
            gain0,
            bias0,
            main.reshape(4 * span, width),
            ffn_sum.reshape(width, 2 * hidden),
            gmerge.reshape(-1, width, gmerge.shape[4]),
            sums,
            tail,
            local,
            head_dim,
            rel,
            win,
        )
    )
    gpb, gain2, bias2, gdb, gain1, bias1 = (x.reshape(width) for x in lines)
    return (
        out.reshape(micro, strip_rows, width),
        grad_input.reshape(micro, strip_rows, wide),
        ggain0.reshape(wide),
        gbias0.reshape(wide),
        gmerge,
        gain1,
        bias1,
        gqkv,
        gqb,
        gtab,
        gproj.reshape(local, head_dim, width),
        gpb,
        gain2,
        bias2,
        gup,
        gub.reshape(hidden),
        gdown,
        gdb,
    )


def solution(mesh):
    placed = (
        P(None, ("dp", "mp"), None),
        P(),
        P(),
        P(),
        P(),
        P(),
        P(None, "mp", None),
        P("mp", None),
        P("mp", None),
        P(),
        P(None, "dp"),
        P(None, "dp"),
        P("mp", None, None),
        P(),
        P(),
        P(),
        P(None, "mp"),
        P("mp"),
        P("mp", None),
        P(),
        P(None, ("dp", "mp"), None),
    )
    return jax.shard_map(
        functools.partial(shards, n_dp=mesh.shape["dp"], n_mp=mesh.shape["mp"]),
        mesh=mesh,
        in_specs=placed,
        out_specs=(
            P(None, ("dp", "mp"), None),
            P(None, ("dp", "mp"), None),
            P(),
            P(),
            P(),
            P(),
            P(),
            P(None, "mp", None),
            P("mp", None),
            P("mp", None),
            P("mp", None, None),
            P(),
            P(),
            P(),
            P(None, "mp"),
            P("mp"),
            P("mp", None),
            P(),
        ),
        check_vma=False,
    )
```

profile of v0, /device:TPU:0, one launch (start us, length us, event | category | flops | bytes accessed | tf_op | source)
XLA Modules:
  0.0 222.9 jit_solution(3656042193456530205)
XLA Ops:
  0.7 0.0 copy-start
  0.7 1.3 copy.45.live_ref
  2.0 1.2 broadcast_in_dim.31.ub_ref
  3.2 0.0 copy-done
  3.2 0.1 constant_dynamic-slice_fusion
  3.3 0.1 reshape.105
  3.4 0.1 constant_dynamic-update-slice_fusion.14
  3.5 0.1 constant_dynamic-update-slice_fusion.13
  3.5 0.1 constant_dynamic-update-slice_fusion.12
  3.6 0.1 constant_dynamic-update-slice_fusion.11
  3.7 0.1 constant_dynamic-update-slice_fusion.10
  3.8 0.1 constant_dynamic-update-slice_fusion.9
  3.8 0.1 constant_dynamic-update-slice_fusion.8
  3.9 0.1 constant_dynamic-update-slice_fusion.6
  4.0 0.1 constant_dynamic-update-slice_fusion.5
  4.1 0.1 constant_dynamic-update-slice_fusion.4
  4.2 0.1 constant_dynamic-update-slice_fusion.3
  4.2 0.1 constant_dynamic-update-slice_fusion.2
  4.3 0.1 constant_dynamic-update-slice_fusion.1
  4.4 0.1 constant_dynamic-update-slice_fusion
  4.5 0.7 tile.9.rid_ref
  5.2 1.8 copy.43.qkvw_ref
  7.0 50.5 %shard_map.340 = (f32[2352,8]{1,0:T(8,128)}, bf16[2352,512]{1,0:T(8,128)(2,1)}, bf16[2352,512]{1,0:T(8,128)(2,1)}, bf16[2352,512]{1,0:T(8,128)(2,1)}, bf16[2352,...) custom-call(bf16[2352,1024]{1,0:T(8,128)(2,1)} %bitcast.101, ...), custom_call_target="tpu_custom_call" | custom-call | flops 24662507520 | bytes 48168960 | tf_op jit(solution)/shard_map/pallas_call | solution.py:43
  57.5 54.8 %shard_map.341 = (bf16[2352,512]{1,0:T(8,128)(2,1)}, bf16[4,2352,512]{2,1,0:T(8,128)(2,1)}, bf16[2352,512]{1,0:T(8,128)(2,1)}, bf16[2352,512]{1,0:T(8,128)(2,1)}...) custom-call(s32[2,1]{1,0:T(2,128)} %copy.45.live_ref, ...), custom_call_target="tpu_custom_call" | custom-call | flops 29595009024 | bytes 24084480 | tf_op jit(solution)/shard_map/pallas_call | solution.py:43
  112.3 93.9 %shard_map.342 = (bf16[2352,512]{1,0:T(8,128)(2,1)}, bf16[2352,1024]{1,0:T(8,128)(2,1)}, bf16[4,128,512]{2,1,0:T(8,128)(2,1)}, bf16[4,64,512]{2,1,0:T(8,128)(2,1...) custom-call(bf16[2352,512]{1,0:T(8,128)(2,1)} %get-tuple-element.62.q_ref, ...), custom_call_target="tpu_custom_call" | custom-call | flops 32061259776 | bytes 24084480 | tf_op jit(solution)/shard_map/pallas_call | solution.py:43
  206.2 0.0 copy-start.1
  206.2 14.5 %shard_map.343 = (f32[2352,512]{1,0:T(8,128)}, f32[2352,1024]{1,0:T(8,128)}, f32[1,1024]{1,0:T(1,128)}, f32[1,1024]{1,0:T(1,128)}, f32[1024,512]{1,0:T(8,128)}, ...) custom-call(s32[2,1]{1,0:T(2,128)} %copy.45.live_ref, ...), custom_call_target="tpu_custom_call" | custom-call | flops 2408448 | bytes 21676032 | tf_op jit(solution)/shard_map/pallas_call | solution.py:43
  220.7 2.0 copy.46
  222.7 0.0 copy-done.1
  (3 shorter events, 0.0 us)
Async XLA Ops:
  0.7 2.5 %copy-start = (s32[2,9408]{1,0:T(2,128)S(1)}, s32[2,9408]{1,0:T(2,128)}, u32[]{:S(2)}) copy-start(s32[2,9408]{1,0:T(2,128)} %param.31) | copy-start | bytes 225796
  206.2 16.5 %copy-start.1 = (s32[2,9408]{1,0:T(2,128)S(1)}, s32[2,9408]{1,0:T(2,128)}, u32[]{:S(2)}) copy-start(s32[2,9408]{1,0:T(2,128)} %param.31) | copy-start | bytes 225796
where the time goes:
time: 222 us; the launch traced here: 223 us
  Pallas kernels  214 us (96%)
  local copies, waits for them, and re-layouts  8.29 us (4%)
    pallas_call x4, Pallas kernels, call(): pl.pallas_call(kernel, grid=(grid,), in_specs=in_specs, out_specs=out_spe...  214 us

commit v1 on v0

--- a/solution.py
+++ b/solution.py
@@ -247,7 +247,7 @@
 
     @pl.when(step == 0)
     def _():
-        own_s[...] = qkvw_ref[...].T
+        own_s[...] = qkvw_ref[...]
         bias = qkvb_ref[...].astype(F32)
         lines = []
         for t in range(3):
@@ -575,13 +575,13 @@
 
 
 def live_rows(live_ref, start, count, rows, width, window):
-    micro = live_ref.shape[0]
+    micro = live_ref.shape[1]
     micro_rows = rows // micro
     before = lax.axis_index("mp") * micro_rows
     row = lax.broadcasted_iota(jnp.int32, (count, width), 0) + start
     live = None
     for m in range(micro):
-        last = m * micro_rows + jnp.minimum(live_ref[m, 0] * window - before, micro_rows)
+        last = m * micro_rows + jnp.minimum(live_ref[0, m] * window - before, micro_rows)
         inside = (row >= m * micro_rows) & (row < last)
         live = inside if live is None else live | inside
     return live
@@ -638,7 +638,7 @@
     pairs = even_s.shape[0]
     pair = pairs - 1 - step
     rows, width = gffn_s.shape
-    blocks = spans(rows, 384)
+    blocks = spans(rows, 512)
     hidden = up_ref.shape[1]
     wp = wp_ref[...].reshape(width, width)
 
@@ -800,7 +800,7 @@
     padded = -(-rows // 128) * 128
     proj_rows = width // size
     proj_at = 2 * hidden // proj_rows
-    blocks = len(spans(rows, 384))
+    blocks = len(spans(rows, 512))
     row_out = jax.ShapeDtypeStruct((rows, width), BF16)
     return call(
         functools.partial(ffn_kernel, local, window),
@@ -1563,31 +1563,56 @@
     live_ref,
     raw_ref,
     gin16_ref,
-    wm_ref,
     g0_ref,
     b0_ref,
-    main_ref,
-    ffn_ref,
-    full_ref,
     sums_ref,
     tail_ref,
+    wm_hbm,
+    main_hbm,
+    ffn_hbm,
+    full_hbm,
     out_ref,
     gin_ref,
     gain0_ref,
     bias0_ref,
-    gmerge_ref,
     gqkv_ref,
     gproj_ref,
-    gup_ref,
-    gdown_ref,
     gqb_ref,
     gtab_ref,
     gub_ref,
-    *line_refs,
+    *rest,
 ):
+    line_refs, rest = rest[:6], rest[6:]
+    gmerge_hbm, gup_hbm, gdown_hbm, wm_ref, main_ref, ffn_ref, full_ref = rest[:7]
+    gmerge_ref, gup_ref, gdown_ref, in_sems, out_sems = rest[7:]
     step = pl.program_id(0)
     count, width = raw_ref.shape
     rows = count * pl.num_programs(0)
+    halves = full_ref.shape[0]
+    narrow = full_ref.shape[2]
+
+    def bring(i):
+        pair = (
+            (main_hbm, main_ref),
+            (ffn_hbm, ffn_ref),
+            (wm_hbm, wm_ref),
+            (full_hbm, full_ref),
+        )[i]
+        return pltpu.make_async_copy(*pair, in_sems.at[i])
+
+    def take(i):
+        if i < 2:
+            pair = ((gup_ref, gup_hbm), (gdown_ref, gdown_hbm))[i]
+        else:
+            here = pl.ds((i - 2) * narrow, narrow)
+            pair = (gmerge_ref.at[here], gmerge_hbm.at[here])
+        return pltpu.make_async_copy(*pair, out_sems.at[i])
+
+    @pl.when(step == 0)
+    def _():
+        for i in range(4):
+            bring(i).start()
+
     live = live_rows(live_ref, step * count, count, rows, width, window)
     out_ref[...] = jnp.where(live, raw_ref[...].astype(F32), 0.0)
     gin_ref[...] = gin16_ref[...].astype(F32)
@@ -1595,15 +1620,12 @@
     @pl.when(step == 0)
     def _():
         span = local * head_dim
+        bring(0).wait()
         main = main_ref[...].astype(F32)
-        order = [
-            main[t * span + l * head_dim : t * span + (l + 1) * head_dim]
-            for l in range(local)
-            for t in range(3)
-        ]
-        grad = jnp.concatenate(order, axis=0).T
         for l in range(local):
-            gqkv_ref[:, l, :] = grad[:, 3 * l * head_dim : 3 * (l + 1) * head_dim]
+            for t in range(3):
+                at = t * span + l * head_dim
+                gqkv_ref[l, t * head_dim : (t + 1) * head_dim, :] = main[at : at + head_dim]
         gproj_ref[...] = main[3 * span :]
         rows_of = []
         for l in range(local):
@@ -1620,12 +1642,16 @@
     @pl.when(step == 1)
     def _():
         hidden = gup_ref.shape[1]
+        bring(1).wait()
         gup_ref[...] = ffn_ref[:, :hidden].astype(F32)
+        take(0).start()
         gdown_ref[...] = ffn_ref[:, hidden:].astype(F32).T
-
-    narrow = full_ref.shape[2]
+        take(1).start()
+        bring(2).wait()
+        bring(3).wait()
+
     low_sum = sums_ref[6:7, :]
-    for j in range(full_ref.shape[0]):
+    for j in range(halves):
 
         @pl.when(step == 2 + j)
         def _():
@@ -1639,6 +1665,12 @@
             scale = jnp.broadcast_to(g0_ref[:, cols], (8, narrow)).T[:, :1]
             offset = jnp.broadcast_to(b0_ref[:, cols], (8, narrow)).T[:, :1]
             gmerge_ref[cols, :] = grad * scale + offset * low_sum
+            take(2 + j).start()
+
+    @pl.when(step == pl.num_programs(0) - 1)
+    def _():
+        for i in range(2 + halves):
+            take(i).wait()
 
 
 def last_rows(
@@ -1651,32 +1683,39 @@
     span = local * head_dim
     narrow_block = pl.BlockSpec((step, width), lambda i: (i, 0))
     wide_block = pl.BlockSpec((step, wide), lambda i: (i, 0))
-    rest = [wm, g0, b0, main, ffn, full, sums, tail]
+    rest = [g0, b0, sums, tail]
+    later = [wm, main, ffn, full]
     shapes = [
         (1, wide),
         (1, wide),
-        (wide, width),
-        (width, local, 3 * head_dim),
+        (local, 3 * head_dim, width),
         (span, width),
-        (width, hidden),
-        (hidden, width),
         (local, 3 * head_dim),
         (local, rel),
         (1, hidden),
     ] + [(1, width)] * 6
+    large = [(wide, width), (width, hidden), (hidden, width)]
     return call(
         functools.partial(last_kernel, head_dim, local, window),
         7,
-        [live, raw, gin16] + rest,
+        [live, raw, gin16] + rest + later,
         [pl.BlockSpec(memory_space=pltpu.SMEM), narrow_block, wide_block]
-        + [whole(a.shape) for a in rest],
+        + [whole(a.shape) for a in rest]
+        + [anywhere()] * len(later),
         [
             jax.ShapeDtypeStruct((rows, width), F32),
             jax.ShapeDtypeStruct((rows, wide), F32),
         ]
-        + [jax.ShapeDtypeStruct(shape, F32) for shape in shapes],
-        [narrow_block, wide_block] + [whole(shape) for shape in shapes],
-        [],
+        + [jax.ShapeDtypeStruct(shape, F32) for shape in shapes + large],
+        [narrow_block, wide_block]
+        + [whole(shape) for shape in shapes]
+        + [anywhere()] * len(large),
+        [pltpu.VMEM(a.shape, BF16) for a in later]
+        + [pltpu.VMEM(shape, F32) for shape in large]
+        + [
+            pltpu.SemaphoreType.DMA((len(later),)),
+            pltpu.SemaphoreType.DMA((2 + full.shape[0],)),
+        ],
         2 * rows * width,
         rows * wide * 9,
     )
@@ -1726,6 +1765,7 @@
     region = jnp.stack([region[:, o * jump : o * jump + COVER] for o in range(TILE)])
     region = jnp.tile(region[:, :, None, :], (1, 1, 1, GROUP))
     table_width = -(-rel // 128) * 128
+    live = live_windows.T
     vecs = (proj_bias[None], norm2_gain[None], norm2_bias[None], down_bias[None])
     gain0, bias0 = norm0_gain[None], norm0_bias[None]
     gain1, bias1 = norm1_gain[None], norm1_bias[None]
@@ -1738,7 +1778,7 @@
         merge_weight,
         gain1,
         bias1,
-        qkv_weight.reshape(width, local * packed),
+        jnp.transpose(qkv_weight, (1, 2, 0)).reshape(local * packed, width),
         qkv_bias,
         rel_table,
         up_bias[None],
@@ -1751,7 +1791,7 @@
         head_dim,
     )
     base, act, gmid, gatt, ffn_part, gub, gproj, sums2 = ffn_rows(
-        live_windows,
+        live,
         n1,
         att,
         cotangent.reshape(rows, width),
@@ -1795,9 +1835,9 @@
         n_dp,
     )
     span = local * head_dim
-    out, grad_input, ggain0, gbias0, gmerge, gqkv, gproj, gup, gdown, gqb, gtab, gub, *lines = (
+    out, grad_input, ggain0, gbias0, gqkv, gproj, gqb, gtab, gub, *lines, gmerge, gup, gdown = (
         last_rows(
-            live_windows,
+            live,
             raw,
             gin16,
             merge_weight,
@@ -1823,7 +1863,7 @@
         gmerge,
         gain1,
         bias1,
-        gqkv,
+        jnp.transpose(gqkv, (2, 0, 1)),
         gqb,
         gtab,
         gproj.reshape(local, head_dim, width),

time: 222 us -> 212 us (0.955)
  Pallas kernels: 214 us -> 208 us
  local copies, waits for them, and re-layouts: 8.29 us -> 3.29 us
    pallas_call x4, Pallas kernels: 214 us -> 208 us  [call(): pl.pallas_call(kernel, grid=(grid,), in_specs=in_specs, out_specs=out_spe...]
    unnamed x21 -> x19, local copies, waits for them, and re-layouts: 4.31 us -> 1.03 us
where the time goes in v1:
time: 212 us; the launch traced here: 213 us
  Pallas kernels  208 us (98%)
  local copies, waits for them, and re-layouts  3.29 us (2%)
    pallas_call x4, Pallas kernels, call(): pl.pallas_call(kernel, grid=(grid,), in_specs=in_specs, out_specs=out_spe...  208 us

profile of v1, /device:TPU:0, one launch (start us, length us, event | category | flops | bytes accessed | tf_op | source)
XLA Modules:
  0.0 212.7 jit_solution(4649551528884686685)
XLA Ops:
  0.7 0.0 copy-start
  0.7 1.3 broadcast_in_dim.31.ub_ref
  1.9 0.0 copy-done
  1.9 0.1 constant_dynamic-slice_fusion
  2.0 0.1 reshape.105
  2.1 0.1 constant_dynamic-update-slice_fusion.14
  2.2 0.1 constant_dynamic-update-slice_fusion.13
  2.3 0.1 constant_dynamic-update-slice_fusion.12
  2.3 0.1 constant_dynamic-update-slice_fusion.11
  2.4 0.1 constant_dynamic-update-slice_fusion.10
  2.5 0.1 constant_dynamic-update-slice_fusion.9
  2.6 0.1 constant_dynamic-update-slice_fusion.8
  2.7 0.1 constant_dynamic-update-slice_fusion.6
  2.7 0.1 constant_dynamic-update-slice_fusion.5
  2.8 0.1 constant_dynamic-update-slice_fusion.4
  2.9 0.1 constant_dynamic-update-slice_fusion.3
  3.0 0.1 constant_dynamic-update-slice_fusion.2
  3.1 0.1 constant_dynamic-update-slice_fusion.1
  3.1 0.1 constant_dynamic-update-slice_fusion
  3.2 0.7 tile.9.rid_ref
  4.0 50.4 %shard_map.340 = (f32[2352,8]{1,0:T(8,128)}, bf16[2352,512]{1,0:T(8,128)(2,1)}, bf16[2352,512]{1,0:T(8,128)(2,1)}, bf16[2352,512]{1,0:T(8,128)(2,1)}, bf16[2352,...) custom-call(bf16[2352,1024]{1,0:T(8,128)(2,1)} %bitcast.106, ...), custom_call_target="tpu_custom_call" | custom-call | flops 24662507520 | bytes 48168960 | tf_op jit(solution)/shard_map/pallas_call | solution.py:43
  54.4 52.2 %shard_map.341 = (bf16[2352,512]{1,0:T(8,128)(2,1)}, bf16[4,2352,512]{2,1,0:T(8,128)(2,1)}, bf16[2352,512]{1,0:T(8,128)(2,1)}, bf16[2352,512]{1,0:T(8,128)(2,1)}...) custom-call(s32[1,2]{1,0:T(1,128)} %bitcast.103, ...), custom_call_target="tpu_custom_call" | custom-call | flops 29595009024 | bytes 24084480 | tf_op jit(solution)/shard_map/pallas_call | solution.py:43
  106.6 93.7 %shard_map.342 = (bf16[2352,512]{1,0:T(8,128)(2,1)}, bf16[2352,1024]{1,0:T(8,128)(2,1)}, bf16[4,128,512]{2,1,0:T(8,128)(2,1)}, bf16[4,64,512]{2,1,0:T(8,128)(2,1...) custom-call(bf16[2352,512]{1,0:T(8,128)(2,1)} %get-tuple-element.62.q_ref, ...), custom_call_target="tpu_custom_call" | custom-call | flops 32061259776 | bytes 24084480 | tf_op jit(solution)/shard_map/pallas_call | solution.py:43
  200.3 0.0 copy-start.1
  200.3 12.2 %shard_map.343 = (f32[2352,512]{1,0:T(8,128)}, f32[2352,1024]{1,0:T(8,128)}, f32[1,1024]{1,0:T(1,128)}, f32[1,1024]{1,0:T(1,128)}, f32[2,96,512]{2,1,0:T(8,128)}...) custom-call(s32[1,2]{1,0:T(1,128)} %bitcast.104, ...), custom_call_target="tpu_custom_call" | custom-call | flops 2408448 | bytes 21676032 | tf_op jit(solution)/shard_map/pallas_call | solution.py:43
  212.5 0.0 copy-done.1
  (3 shorter events, 0.0 us)
Async XLA Ops:
  0.7 1.3 copy-start
  200.3 12.2 %copy-start.1 = (s32[2,9408]{1,0:T(2,128)S(1)}, s32[2,9408]{1,0:T(2,128)}, u32[]{:S(2)}) copy-start(s32[2,9408]{1,0:T(2,128)} %param.31) | copy-start | bytes 225796

commit v2 on v1

--- a/solution.py
+++ b/solution.py
@@ -256,7 +256,9 @@
             ]
             lines.append(fill(jnp.concatenate(parts, axis=1), width))
         lines.append(fill(tab_ref[...].astype(F32), width))
-        lines.append(fill(ub_ref[...].astype(F32), width))
+        up_bias = ub_ref[...].astype(F32)
+        parts = [up_bias[i : i + 1, :] for i in range(up_bias.shape[0])]
+        lines.append(fill(jnp.concatenate(parts, axis=1), width))
         lines.append(jnp.zeros((TILE - 4 - local, width), F32))
         tile_s[...] = jnp.concatenate(lines, axis=0).astype(BF16)
         greet([("mp", r) for r in range(1, size)])
@@ -927,7 +929,6 @@
     gtab_s,
     ffncame_s,
     ffnown_s,
-    merge_s,
     merged_s,
     mnear_s,
     mfar_s,
@@ -1224,7 +1225,6 @@
     def _():
         for c in bring_late():
             c.start()
-        merge_s[...] = jnp.zeros_like(merge_s)
         lines_s[...] = jnp.zeros_like(lines_s)
         for c in bring_more():
             c.wait()
@@ -1242,7 +1242,7 @@
         for c in pnear:
             c.start()
 
-    @pl.when(step == TILE + 2)
+    @pl.when(step == TILE + 1)
     def _():
         for p in reversed(range(pairs)):
             pnear[p].wait_recv()
@@ -1272,15 +1272,15 @@
         normed0 = ((x_ref[...].astype(F32) - stats[:, 0:1]) * stats[:, 1:2]).astype(BF16)
         n0_s[here, :] = normed0
         inv0_s[here, :] = jnp.broadcast_to(stats[:, 1:2], (count, inv0_s.shape[1]))
-        merge_s[...] += dot_lt(grad_merged, normed0)
 
     @pl.when(step == TILE + dense_steps - 1)
     def _():
         narrow = merged_s.shape[1]
-        per_half = merge_s.shape[1] // narrow // halves
+        per_half = n0_s.shape[1] // narrow // halves
+        merged_t = q_s[...].T
         for h in range(halves):
             for j in range(h * per_half, (h + 1) * per_half):
-                part = merge_s[:, j * narrow : (j + 1) * narrow]
+                part = dot(merged_t, n0_s[:, j * narrow : (j + 1) * narrow])
                 merged_s[j * width : (j + 1) * width, :] = part.astype(BF16)
             for c in mnear[h]:
                 c.start()
@@ -1318,8 +1318,6 @@
         lineout_s[0] = total
         for c in lines_out:
             c.start()
-        input_part(0)
-
         total = parts_s[0].astype(F32)
         for p in reversed(range(1, pairs)):
             pfar[p].wait_recv()
@@ -1327,6 +1325,8 @@
         parts_s[0] = total.astype(BF16)
         for c in main_out:
             c.start()
+        input_part(0)
+
         for h in range(halves):
             mine = pl.ds(pl.multiple_of(share_at(h, me), TILE), share)
             total = merged_s[mine, :].astype(F32)
@@ -1368,7 +1368,7 @@
             keep_merge(h).wait()
             for c in back[h]:
                 c.wait_recv()
-            for c in spread[h]:
+            for c in spread[h][-1:] + spread[h][-2::-1]:
                 c.start()
         total = tparts_s[0].astype(F32)
         for p in reversed(range(1, pairs)):
@@ -1523,7 +1523,6 @@
             pltpu.VMEM((heads, table_width), F32),
             pltpu.VMEM((far_size,) + piece, BF16),
             pltpu.VMEM(piece, BF16),
-            pltpu.VMEM((width, wide), F32),
             pltpu.VMEM((total_rows, narrow), BF16),
             pltpu.VMEM((halves, pairs, share, narrow), BF16),
             pltpu.VMEM((halves, pairs, share, narrow), BF16),
@@ -1781,7 +1780,7 @@
         jnp.transpose(qkv_weight, (1, 2, 0)).reshape(local * packed, width),
         qkv_bias,
         rel_table,
-        up_bias[None],
+        up_bias.reshape(-1, 128),
         up_weight,
         down_weight,
         proj_weight.reshape(local * head_dim, width),

time: 212 us -> 209 us (0.986)
  no operation moved by 1% of the time
where the time goes in v2:
time: 209 us; the launch traced here: 211 us
  Pallas kernels  207 us (99%)
  local copies, waits for them, and re-layouts  2.91 us (1%)
    pallas_call x4, Pallas kernels, call(): pl.pallas_call(kernel, grid=(grid,), in_specs=in_specs, out_specs=out_spe...  207 us

profile of v2, /device:TPU:0, one launch (start us, length us, event | category | flops | bytes accessed | tf_op | source)
XLA Modules:
  0.0 210.7 jit_solution(12888722883827938277)
XLA Ops:
  0.7 0.0 copy-start
  0.7 0.9 copy-done
  1.5 0.1 constant_dynamic-slice_fusion
  1.6 0.1 reshape.109
  1.7 0.1 constant_dynamic-update-slice_fusion.14
  1.8 0.1 constant_dynamic-update-slice_fusion.13
  1.9 0.1 constant_dynamic-update-slice_fusion.12
  2.0 0.1 constant_dynamic-update-slice_fusion.11
  2.0 0.1 constant_dynamic-update-slice_fusion.10
  2.1 0.1 constant_dynamic-update-slice_fusion.9
  2.2 0.1 constant_dynamic-update-slice_fusion.8
  2.3 0.1 constant_dynamic-update-slice_fusion.6
  2.4 0.1 constant_dynamic-update-slice_fusion.5
  2.4 0.1 constant_dynamic-update-slice_fusion.4
  2.5 0.1 constant_dynamic-update-slice_fusion.3
  2.6 0.1 constant_dynamic-update-slice_fusion.2
  2.7 0.1 constant_dynamic-update-slice_fusion.1
  2.8 0.1 constant_dynamic-update-slice_fusion
  2.9 0.7 tile.9.rid_ref
  3.6 50.4 %shard_map.340 = (f32[2352,8]{1,0:T(8,128)}, bf16[2352,512]{1,0:T(8,128)(2,1)}, bf16[2352,512]{1,0:T(8,128)(2,1)}, bf16[2352,512]{1,0:T(8,128)(2,1)}, bf16[2352,...) custom-call(bf16[2352,1024]{1,0:T(8,128)(2,1)} %bitcast.107, ...), custom_call_target="tpu_custom_call" | custom-call | flops 24662507520 | bytes 48168960 | tf_op jit(solution)/shard_map/pallas_call | solution.py:43
  54.0 52.2 %shard_map.341 = (bf16[2352,512]{1,0:T(8,128)(2,1)}, bf16[4,2352,512]{2,1,0:T(8,128)(2,1)}, bf16[2352,512]{1,0:T(8,128)(2,1)}, bf16[2352,512]{1,0:T(8,128)(2,1)}...) custom-call(s32[1,2]{1,0:T(1,128)} %bitcast.104, ...), custom_call_target="tpu_custom_call" | custom-call | flops 29595009024 | bytes 24084480 | tf_op jit(solution)/shard_map/pallas_call | solution.py:43
  106.2 92.0 %shard_map.342 = (bf16[2352,512]{1,0:T(8,128)(2,1)}, bf16[2352,1024]{1,0:T(8,128)(2,1)}, bf16[4,128,512]{2,1,0:T(8,128)(2,1)}, bf16[4,64,512]{2,1,0:T(8,128)(2,1...) custom-call(bf16[2352,512]{1,0:T(8,128)(2,1)} %get-tuple-element.62.q_ref, ...), custom_call_target="tpu_custom_call" | custom-call | flops 32061259776 | bytes 24084480 | tf_op jit(solution)/shard_map/pallas_call | solution.py:43
  198.2 0.0 copy-start.1
  198.2 12.2 %shard_map.343 = (f32[2352,512]{1,0:T(8,128)}, f32[2352,1024]{1,0:T(8,128)}, f32[1,1024]{1,0:T(1,128)}, f32[1,1024]{1,0:T(1,128)}, f32[2,96,512]{2,1,0:T(8,128)}...) custom-call(s32[1,2]{1,0:T(1,128)} %bitcast.105, ...), custom_call_target="tpu_custom_call" | custom-call | flops 2408448 | bytes 21676032 | tf_op jit(solution)/shard_map/pallas_call | solution.py:43
  210.4 0.0 copy-done.1
  (3 shorter events, 0.0 us)
Async XLA Ops:
  0.7 0.9 copy-start
  198.2 12.2 %copy-start.1 = (s32[2,9408]{1,0:T(2,128)S(1)}, s32[2,9408]{1,0:T(2,128)}, u32[]{:S(2)}) copy-start(s32[2,9408]{1,0:T(2,128)} %param.31) | copy-start | bytes 225796

commit v3 on v2

--- a/solution.py
+++ b/solution.py
@@ -1652,7 +1652,7 @@
     low_sum = sums_ref[6:7, :]
     for j in range(halves):
 
-        @pl.when(step == 2 + j)
+        @pl.when(step == 1 + 2 * j // halves)
         def _():
             cols = pl.ds(j * narrow, narrow)
             grad = full_ref[j].astype(F32).T
@@ -1677,7 +1677,7 @@
 ):
     rows, width = raw.shape
     wide = gin16.shape[1]
-    step = rows // 7
+    step = rows // 3
     hidden = ffn.shape[1] // 2
     span = local * head_dim
     narrow_block = pl.BlockSpec((step, width), lambda i: (i, 0))
@@ -1696,7 +1696,7 @@
     large = [(wide, width), (width, hidden), (hidden, width)]
     return call(
         functools.partial(last_kernel, head_dim, local, window),
-        7,
+        3,
         [live, raw, gin16] + rest + later,
         [pl.BlockSpec(memory_space=pltpu.SMEM), narrow_block, wide_block]
         + [whole(a.shape) for a in rest]

time: 209 us -> 208 us (level)
  no operation moved by 1% of the time
where the time goes in v3:
time: 208 us; the launch traced here: 210 us
  Pallas kernels  206 us (99%)
  local copies, waits for them, and re-layouts  2.91 us (1%)
    pallas_call x4, Pallas kernels, call(): pl.pallas_call(kernel, grid=(grid,), in_specs=in_specs, out_specs=out_spe...  206 us

profile of v3, /device:TPU:0, one launch (start us, length us, event | category | flops | bytes accessed | tf_op | source)
XLA Modules:
  0.0 210.0 jit_solution(5179419565365647616)
XLA Ops:
  0.7 0.0 copy-start
  0.7 0.9 copy-done
  1.5 0.1 constant_dynamic-slice_fusion
  1.6 0.1 reshape.109
  1.7 0.1 constant_dynamic-update-slice_fusion.14
  1.8 0.1 constant_dynamic-update-slice_fusion.13
  1.9 0.1 constant_dynamic-update-slice_fusion.12
  2.0 0.1 constant_dynamic-update-slice_fusion.11
  2.0 0.1 constant_dynamic-update-slice_fusion.10
  2.1 0.1 constant_dynamic-update-slice_fusion.9
  2.2 0.1 constant_dynamic-update-slice_fusion.8
  2.3 0.1 constant_dynamic-update-slice_fusion.6
  2.4 0.1 constant_dynamic-update-slice_fusion.5
  2.4 0.1 constant_dynamic-update-slice_fusion.4
  2.5 0.1 constant_dynamic-update-slice_fusion.3
  2.6 0.1 constant_dynamic-update-slice_fusion.2
  2.7 0.1 constant_dynamic-update-slice_fusion.1
  2.8 0.1 constant_dynamic-update-slice_fusion
  2.9 0.7 tile.9.rid_ref
  3.6 50.4 %shard_map.340 = (f32[2352,8]{1,0:T(8,128)}, bf16[2352,512]{1,0:T(8,128)(2,1)}, bf16[2352,512]{1,0:T(8,128)(2,1)}, bf16[2352,512]{1,0:T(8,128)(2,1)}, bf16[2352,...) custom-call(bf16[2352,1024]{1,0:T(8,128)(2,1)} %bitcast.107, ...), custom_call_target="tpu_custom_call" | custom-call | flops 24662507520 | bytes 48168960 | tf_op jit(solution)/shard_map/pallas_call | solution.py:43
  54.0 52.2 %shard_map.341 = (bf16[2352,512]{1,0:T(8,128)(2,1)}, bf16[4,2352,512]{2,1,0:T(8,128)(2,1)}, bf16[2352,512]{1,0:T(8,128)(2,1)}, bf16[2352,512]{1,0:T(8,128)(2,1)}...) custom-call(s32[1,2]{1,0:T(1,128)} %bitcast.104, ...), custom_call_target="tpu_custom_call" | custom-call | flops 29595009024 | bytes 24084480 | tf_op jit(solution)/shard_map/pallas_call | solution.py:43
  106.2 92.0 %shard_map.342 = (bf16[2352,512]{1,0:T(8,128)(2,1)}, bf16[2352,1024]{1,0:T(8,128)(2,1)}, bf16[4,128,512]{2,1,0:T(8,128)(2,1)}, bf16[4,64,512]{2,1,0:T(8,128)(2,1...) custom-call(bf16[2352,512]{1,0:T(8,128)(2,1)} %get-tuple-element.62.q_ref, ...), custom_call_target="tpu_custom_call" | custom-call | flops 32061259776 | bytes 24084480 | tf_op jit(solution)/shard_map/pallas_call | solution.py:43
  198.2 0.0 copy-start.1
  198.2 11.5 %shard_map.343 = (f32[2352,512]{1,0:T(8,128)}, f32[2352,1024]{1,0:T(8,128)}, f32[1,1024]{1,0:T(1,128)}, f32[1,1024]{1,0:T(1,128)}, f32[2,96,512]{2,1,0:T(8,128)}...) custom-call(s32[1,2]{1,0:T(1,128)} %bitcast.105, ...), custom_call_target="tpu_custom_call" | custom-call | flops 2408448 | bytes 21676032 | tf_op jit(solution)/shard_map/pallas_call | solution.py:43
  209.8 0.0 copy-done.1
  (3 shorter events, 0.0 us)
Async XLA Ops:
  0.7 0.9 copy-start
  198.2 11.5 %copy-start.1 = (s32[2,9408]{1,0:T(2,128)S(1)}, s32[2,9408]{1,0:T(2,128)}, u32[]{:S(2)}) copy-start(s32[2,9408]{1,0:T(2,128)} %param.31) | copy-start | bytes 225796
